TPU v7x, 256 devices: a whole 4x4x8 slice. The times are simulated.
256 devices in a mesh: lat: 16 (over z, y_lo), lon: 16 (over x, y_hi, core).
Axes of the slice: x: 4, y: 4 (y_hi: 2, y_lo: 2; y = y_hi * 2 + y_lo), z: 8, core: 2. Of those that a mesh axis runs over, the one named last changes fastest.
Arguments:
- features: bfloat16 [256, 512, 512], P('lat', 'lon'), may hold values from -6 to 6
- land_mask: int32 [256, 512], P('lat', 'lon'), may hold values 0 or 1
- land_embed: float32 [512], replicated, may hold values from -4 to 4
- window_shift: int32 [1], replicated, may hold values from 1 to 15
- fine_gain: float32 [512], replicated, may hold values from 0.5 to 1.5
- qkv_weight: bfloat16 [512, 1536], replicated, may hold values from -0.25 to 0.25
- bias_table: float32 [8, 465], replicated, may hold values from -4 to 400
- mix_weight: bfloat16 [512, 512], replicated, may hold values from -0.25 to 0.25
- merge_gain: float32 [2048], replicated, may hold values from 0.5 to 1.5
- merge_weight: bfloat16 [2048, 1024], replicated, may hold values from -0.125 to 0.125
- coarse_gain: float32 [1024], replicated, may hold values from 0.5 to 1.5
- inner_weight: bfloat16 [1024, 4096], P(None, 'lon'), may hold values from -0.1875 to 0.1875
- outer_weight: bfloat16 [4096, 1024], P('lon'), may hold values from -0.09375 to 0.09375
- expand_weight: bfloat16 [1024, 2048], replicated, may hold values from -0.1875 to 0.1875
- cotangent: bfloat16 [256, 512, 512], P('lat', 'lon'), may hold values from -0.25 to 0.25
Outputs:
- prediction: bfloat16 [256, 512, 512], P('lat', 'lon')
- grad_inner: float32 [1024, 4096], P('lat', 'lon')
- grad_outer: float32 [4096, 1024], P('lon', 'lat')
All inputs are finite; a program needn't handle non-finite values. No bound on the sum of `land_mask` on one device may be relied on, other than what follows from the above.
Results may differ from a plain program's by a relative error of at most 0.03.
Values may be sent and summed in bfloat16 or wider, within the bound.
A program may use at most 128 MiB of HBM per device.

v0:
```python
import jax
import jax.numpy as jnp
from jax import lax
from jax.sharding import PartitionSpec as P

HEADS1 = 8
WH = 8
WL = 16


NORM_EPS = 1e-05
GELU_SCALE = 0.7978845608028654


def with_halo(cells, sides, width):
    for axis, dim in sides:
        count = lax.axis_size(axis)
        head = lax.slice_in_dim(cells, 0, width, axis=dim)
        tail = lax.slice_in_dim(cells, cells.shape[dim] - width, cells.shape[dim], axis=dim)
        cells = jnp.concatenate(
            [
                lax.ppermute(tail, axis, [(i, (i + 1) % count) for i in range(count)]),
                cells,
                lax.ppermute(head, axis, [((i + 1) % count, i) for i in range(count)]),
            ],
            axis=dim,
        )
    return cells


def layer_norm(values, gain):
    centre = jnp.mean(values, axis=-1, keepdims=True)
    centred = values - centre
    spread = jnp.mean(centred * centred, axis=-1, keepdims=True)
    return centred * lax.rsqrt(spread + NORM_EPS) * gain


def gelu_pair(pre_act):
    inner = GELU_SCALE * (pre_act + 0.044715 * pre_act * pre_act * pre_act)
    tangent = jnp.tanh(inner)
    value = 0.5 * pre_act * (1.0 + tangent)
    slope = 0.5 * (1.0 + tangent) + 0.5 * pre_act * (1.0 - tangent * tangent) * GELU_SCALE * (
        1.0 + 3.0 * 0.044715 * pre_act * pre_act
    )
    return (value, slope)


def bias_matrix(bias_table, win_rows, win_cols):
    places = jnp.arange(win_rows * win_cols, dtype=jnp.int32)
    place_row = places // win_cols
    place_col = places % win_cols
    lookup = (place_row[:, None] - place_row[None, :] + win_rows - 1) * (2 * win_cols - 1) + (
        place_col[:, None] - place_col[None, :] + win_cols - 1
    )
    return bias_table[:, lookup]


def window_attention(normed, qkv_weight, position_bias, win_rows, win_cols, head_count):
    grid_rows, grid_cols, feat_width = normed.shape
    window_size = win_rows * win_cols
    head_size = feat_width // head_count
    windows = normed.reshape(
        grid_rows // win_rows, win_rows, grid_cols // win_cols, win_cols, feat_width
    )
    windows = windows.transpose(0, 2, 1, 3, 4).reshape(-1, window_size, feat_width)
    projected = jnp.dot(windows, qkv_weight, preferred_element_type=jnp.float32).astype(
        jnp.bfloat16
    )
    projected = projected.reshape(windows.shape[0], window_size, 3, head_count, head_size)
    queries = projected[:, :, 0]
    key_rows = projected[:, :, 1]
    values = projected[:, :, 2]
    scores = (
        jnp.einsum("nqhd,nkhd->nhqk", queries, key_rows, preferred_element_type=jnp.float32)
        * head_size ** (-0.5)
        + position_bias[None]
    )
    row_max = jnp.max(scores, axis=-1, keepdims=True)
    expo = jnp.exp(scores - row_max)
    prob_rows = (expo / jnp.sum(expo, axis=-1, keepdims=True)).astype(jnp.bfloat16)
    attended = jnp.einsum(
        "nhqk,nkhd->nqhd", prob_rows, values, preferred_element_type=jnp.float32
    ).astype(jnp.bfloat16)
    attended = attended.reshape(
        grid_rows // win_rows, grid_cols // win_cols, win_rows, win_cols, feat_width
    )
    return attended.transpose(0, 2, 1, 3, 4).reshape(grid_rows, grid_cols, feat_width)


def fold_quads(grid):
    grid_rows, grid_cols, feat_width = grid.shape
    folded = grid.reshape(grid_rows // 2, 2, grid_cols // 2, 2, feat_width).transpose(0, 2, 1, 3, 4)
    return folded.reshape(grid_rows // 2, grid_cols // 2, 4 * feat_width)


def unfold_quads(grid, feat_width):
    grid_rows, grid_cols, total_width = grid.shape
    spread_out = grid.reshape(grid_rows, grid_cols, 2, 2, feat_width).transpose(0, 2, 1, 3, 4)
    return spread_out.reshape(grid_rows * 2, grid_cols * 2, feat_width)


def local(
    features,
    land_mask,
    land_embed,
    window_shift,
    fine_gain,
    qkv_weight,
    bias_table,
    mix_weight,
    merge_gain,
    merge_weight,
    coarse_gain,
    inner_weight,
    outer_weight,
    expand_weight,
    cotangent,
):
    tile_rows, tile_cols, feat_width = features.shape
    offset = window_shift[0]
    position_bias = bias_matrix(bias_table, WH, WL)
    base_rows = features.astype(jnp.float32) + land_mask.astype(jnp.float32)[..., None] * land_embed
    normed = layer_norm(base_rows, fine_gain).astype(jnp.bfloat16)
    widened = with_halo(normed, (("lon", 1),), WL)
    chosen = lax.dynamic_slice_in_dim(widened, offset, tile_cols + WL, 1)
    attended_wide = window_attention(chosen, qkv_weight, position_bias, WH, WL, HEADS1)
    attended = lax.dynamic_slice_in_dim(attended_wide, WL - offset, tile_cols, 1)
    level_one = (
        base_rows + jnp.dot(attended, mix_weight, preferred_element_type=jnp.float32)
    ).astype(jnp.bfloat16)
    merged = layer_norm(fold_quads(level_one).astype(jnp.float32), merge_gain).astype(jnp.bfloat16)
    coarse_cells = jnp.dot(
        merged.reshape(-1, 4 * feat_width), merge_weight, preferred_element_type=jnp.float32
    ).astype(jnp.bfloat16)
    lifted = layer_norm(coarse_cells.astype(jnp.float32), coarse_gain).astype(jnp.bfloat16)
    lifted_all = lax.all_gather(lifted, "lon", axis=0, tiled=True)
    pre_all = jnp.dot(lifted_all, inner_weight, preferred_element_type=jnp.float32)
    value_all, slope_all = gelu_pair(pre_all)
    hidden_all = value_all.astype(jnp.bfloat16)
    update = lax.psum_scatter(
        jnp.dot(hidden_all, outer_weight, preferred_element_type=jnp.float32).astype(jnp.bfloat16),
        "lon",
        scatter_dimension=0,
        tiled=True,
    ).astype(jnp.float32)
    back_cells = (coarse_cells.astype(jnp.float32) + update).astype(jnp.bfloat16)
    raised = jnp.dot(back_cells, expand_weight, preferred_element_type=jnp.float32).reshape(
        tile_rows // 2, tile_cols // 2, 4 * feat_width
    )
    prediction = (level_one.astype(jnp.float32) + unfold_quads(raised, feat_width)).astype(
        jnp.bfloat16
    )
    cot_folded = fold_quads(cotangent).reshape(-1, 4 * feat_width)
    cot_coarse = lax.dot_general(
        cot_folded, expand_weight, (((1,), (1,)), ((), ())), preferred_element_type=jnp.float32
    ).astype(jnp.bfloat16)
    cot_all = lax.all_gather(cot_coarse, "lon", axis=0, tiled=True)
    cot_hidden = lax.dot_general(
        cot_all, outer_weight, (((1,), (1,)), ((), ())), preferred_element_type=jnp.float32
    )
    cot_pre = (cot_hidden * slope_all).astype(jnp.bfloat16)
    term_inner = lax.dot_general(
        lifted_all, cot_pre, (((0,), (0,)), ((), ())), preferred_element_type=jnp.float32
    )
    term_outer = lax.dot_general(
        hidden_all, cot_all, (((0,), (0,)), ((), ())), preferred_element_type=jnp.float32
    )
    grad_inner, grad_outer = (
        lax.psum_scatter(
            term_inner.astype(jnp.bfloat16), "lat", scatter_dimension=0, tiled=True
        ).astype(jnp.float32),
        lax.psum_scatter(
            term_outer.astype(jnp.bfloat16), "lat", scatter_dimension=1, tiled=True
        ).astype(jnp.float32),
    )
    return (prediction, grad_inner, grad_outer)


def solution(mesh):
    return jax.shard_map(
        local,
        mesh=mesh,
        in_specs=(
            P("lat", "lon", None),
            P("lat", "lon"),
            P(),
            P(),
            P(),
            P(),
            P(),
            P(),
            P(),
            P(),
            P(),
            P(None, "lon"),
            P("lon", None),
            P(),
            P("lat", "lon", None),
        ),
        out_specs=(P("lat", "lon", None), P("lat", "lon"), P("lon", "lat")),
        check_vma=False,
    )
```

profile of v0, /device:TPU:8, one launch (start us, length us, event | category | flops | bytes accessed | tf_op | source)
XLA Modules:
  0.0 490.6 jit_solution(9286402582971272492)
XLA Ops:
  8.0 1.3 fusion.18
  9.4 1.5 multiply_reduce_fusion.1
  10.9 1.4 multiply_convert_fusion.2
  13.0 5.4 %collective-permute-start.1 = (bf16[16,16,512]{2,1,0:T(8,128)(2,1)S(1)}, bf16[16,16,512]{2,1,0:T(8,128)(2,1)S(1)}, u32[]{:S(2)}, u32[]{:S(2)}) collective-permute-start(bf16[16,16,512]{2,1,0:T(8,128)(2,1)S(1)} %get-tuple-element.3), channel_id=1, source_target_pairs={{1,0},{2,1},{3,2},{4,3},{5,4},{6,5},{7,6},{8,7},{9,8},{10,9},{11,1... | collective-permute-start | bytes 786440 | tf_op jit(solution)/shard_map/ppermute | solution.py:24
  19.3 54.4 %gather_fusion = f32[16384,8]{1,0:T(8,128)} fusion(f32[8,465]{0,1:T(8,128)S(1)} %copy.31, s32[16384]{0:T(1024)S(1)} %fusion.29), kind=kCustom, calls=%fused_computation | custom fusion | bytes 1114112 | tf_op jit(solution)/shard_map/gather | solution.py:55
  73.7 6.7 %copy.32 = f32[128,128,8]{0,1,2:T(8,128)S(1)} copy(f32[128,128,8]{2,1,0:T(8,128)} %bitcast.69) | data formatting | bytes 1048576 | tf_op jit(solution)/shard_map/gather | solution.py:55
  81.1 2.8 convolution_convert_fusion.1
  83.9 4.3 copy.27
  88.2 2.0 fusion.21
  90.2 1.1 fusion.39
  91.2 1.7 fusion.13
  95.0 1.5 fusion.15
  97.5 1.4 copy.51
  99.9 2.1 reshape.252
  102.1 3.1 fusion.40
  107.5 4.5 convolution_convert_fusion.4
  112.1 55.3 %all-gather.3.cloned.1.call-done = bf16[2048,1024]{1,0:T(8,128)(2,1)} async-done(((bf16[128,1024]{1,0:T(8,128)(2,1)}), bf16[2048,1024]{1,0:T(8,128)(2,1)}) %all-gather.3.cloned.1.call-update) | async-done | bytes 4194320 | tf_op jit(solution)/shard_map/all_gather | solution.py:136
  167.4 4.8 fusion.41
  172.2 57.9 %all-gather.5.cloned.1.call-done = bf16[2048,1024]{1,0:T(8,128)(2,1)} async-done(((bf16[128,1024]{1,0:T(8,128)(2,1)}), bf16[2048,1024]{1,0:T(8,128)(2,1)}) %all-gather.5.cloned.1.call-update) | async-done | bytes 4194320 | tf_op jit(solution)/shard_map/all_gather | solution.py:157
  230.1 9.7 %convolution_convert_fusion.3 = bf16[1024,256]{1,0:T(8,128)(2,1)} fusion(bf16[2048,1024]{1,0:T(8,128)(2,1)} %all-gather.3.cloned.1.call-done, bf16[2048,1024]{1,0:T(8,128)(2,1)} %all-gather.5.cloned.1.call-done, bf16[256,1024]{1,0:T(8,128)(2,1)S(1)} %copy-done.9, f32[2048,256]{1,0:T(8,128)} %fusion.41), kind=kOutput, calls=%fused_computation.28 | convolution fusion | flops 2157707264 | bytes 11534336 | tf_op jit(solution)/shard_map/dot_general | solution.py:162
  239.9 5.7 %convolution_convert_fusion.2 = bf16[256,1024]{0,1:T(8,128)(2,1)} fusion(bf16[2048,1024]{1,0:T(8,128)(2,1)} %all-gather.5.cloned.1.call-done, f32[2048,256]{1,0:T(8,128)} %fusion.41), kind=kOutput, calls=%fused_computation.27 | convolution fusion | flops 1078722560 | bytes 6815744 | tf_op jit(solution)/shard_map/dot_general | solution.py:165
  245.9 5.0 %convolution_convert_fusion = bf16[2048,1024]{1,0:T(8,128)(2,1)} fusion(bf16[256,1024]{1,0:T(8,128)(2,1)S(1)} %copy-done.9, f32[2048,256]{1,0:T(8,128)} %fusion.41), kind=kOutput, calls=%fused_computation.2 | convolution fusion | flops 1080557568 | bytes 6815744 | tf_op jit(solution)/shard_map/dot_general | solution.py:141
  250.9 56.2 %reduce-scatter.6.cloned.1.call-done = bf16[64,256]{1,0:T(8,128)(2,1)} async-done(((bf16[1024,256]{1,0:T(8,128)(2,1)}), bf16[64,256]{1,0:T(8,128)(2,1)}) %reduce-scatter.6.cloned.1.call-update) | async-done | bytes 32784 | tf_op jit(solution)/shard_map/reduce_scatter | solution.py:169
  307.0 1.4 convert_element_type.119
  308.4 70.0 %reduce-scatter.8.cloned.1.call-done = bf16[256,64]{0,1:T(8,128)(2,1)} async-done(((bf16[256,1024]{0,1:T(8,128)(2,1)}), bf16[256,64]{0,1:T(8,128)(2,1)}) %reduce-scatter.8.cloned.1.call-update) | async-done | bytes 32784 | tf_op jit(solution)/shard_map/reduce_scatter | solution.py:172
  378.4 1.4 convert_element_type.121
  379.8 91.5 %reduce-scatter.4.cloned.1.call-done = bf16[128,1024]{1,0:T(8,128)(2,1)} async-done(((bf16[2048,1024]{1,0:T(8,128)(2,1)}), bf16[128,1024]{1,0:T(8,128)(2,1)}) %reduce-scatter.4.cloned.1.call-update) | async-done | bytes 262160 | tf_op jit(solution)/shard_map/reduce_scatter | solution.py:140
  471.2 4.0 fusion.27
  475.2 2.1 reshape_reshape.6
  477.4 1.5 copy.50
  478.8 3.1 reshape.250
  481.9 2.2 add_convert_fusion
  (59 shorter events, 9.3 us)
Async XLA Ops:
  7.2 73.9 %copy-start = (bf16[512,1536]{1,0:T(8,128)(2,1)S(1)}, bf16[512,1536]{1,0:T(8,128)(2,1)}, u32[]{:S(2)}) copy-start(bf16[512,1536]{1,0:T(8,128)(2,1)} %param.20) | copy-start | bytes 4718596
  7.2 11.8 %copy-start.5 = (f32[8,465]{1,0:T(8,128)S(1)}, f32[8,465]{1,0:T(8,128)}, u32[]{:S(2)}) copy-start(f32[8,465]{1,0:T(8,128)} %param.21) | copy-start | bytes 44644
  7.2 160.2 %all-gather.3.cloned.1.call-start = ((), (), s32[]{:S(2)}) async-start(), calls=%async_computation.3 | async-start | bytes 4456448 | tf_op jit(solution)/shard_map/all_gather | solution.py:136
  13.0 67.4 %collective-permute-start = (bf16[16,16,512]{2,1,0:T(8,128)(2,1)}, bf16[16,16,512]{2,1,0:T(8,128)(2,1)S(1)}, u32[]{:S(2)}, u32[]{:S(2)}) collective-permute-start(bf16[16,16,512]{2,1,0:T(8,128)(2,1)} %get-tuple-element.4), channel_id=1, source_target_pairs={{0,1},{1,2},{2,3},{3,4},{4,5},{5,6},{6,7},{7,8},{8,9},{9,10},{10,1... | collective-permute-start | bytes 786440 | tf_op jit(solution)/shard_map/ppermute | solution.py:22
  13.0 67.4 %collective-permute-start.1 = (bf16[16,16,512]{2,1,0:T(8,128)(2,1)S(1)}, bf16[16,16,512]{2,1,0:T(8,128)(2,1)S(1)}, u32[]{:S(2)}, u32[]{:S(2)}) collective-permute-start(bf16[16,16,512]{2,1,0:T(8,128)(2,1)S(1)} %get-tuple-element.3), channel_id=1, source_target_pairs={{1,0},{2,1},{3,2},{4,3},{5,4},{6,5},{7,6},{8,7},{9,8},{10,9},{11,1... | collective-permute-start | bytes 786440 | tf_op jit(solution)/shard_map/ppermute | solution.py:24
  93.9 1.1 copy-start.2
  93.9 1.1 copy-start.4
  98.9 3.2 copy-start.6
  102.0 3.3 copy-start.7
  102.0 4.5 copy-start.3
  106.2 123.9 %all-gather.5.cloned.1.call-start = ((), (), s32[]{:S(2)}) async-start(), calls=%async_computation.5 | async-start | bytes 4456448 | tf_op jit(solution)/shard_map/all_gather | solution.py:157
  107.5 59.9 %copy-start.8 = (bf16[1024,256]{1,0:T(8,128)(2,1)S(1)}, bf16[1024,256]{1,0:T(8,128)(2,1)}, u32[]{:S(2)}) copy-start(bf16[1024,256]{1,0:T(8,128)(2,1)} %param.26) | copy-start | bytes 1572868
  112.0 118.1 %copy-start.9 = (bf16[256,1024]{1,0:T(8,128)(2,1)S(1)}, bf16[256,1024]{1,0:T(8,128)(2,1)}, u32[]{:S(2)}) copy-start(bf16[256,1024]{1,0:T(8,128)(2,1)} %param.27) | copy-start | bytes 1572868
  112.0 195.0 %reduce-scatter.6.cloned.1.call-start = ((), (), s32[]{:S(2)}) async-start(), calls=%async_computation.6 | async-start | bytes 557056 | tf_op jit(solution)/shard_map/reduce_scatter | solution.py:169
  239.8 138.6 %reduce-scatter.8.cloned.1.call-start = ((), (), s32[]{:S(2)}) async-start(), calls=%async_computation.7 | async-start | bytes 557056 | tf_op jit(solution)/shard_map/reduce_scatter | solution.py:172
  245.6 225.7 %reduce-scatter.4.cloned.1.call-start = ((), (), s32[]{:S(2)}) async-start(), calls=%async_computation.4 | async-start | bytes 4456448 | tf_op jit(solution)/shard_map/reduce_scatter | solution.py:140
  478.8 5.3 %copy-start.1 = (bf16[512,1536]{1,0:T(8,128)(2,1)S(1)}, bf16[512,1536]{1,0:T(8,128)(2,1)}, u32[]{:S(2)}) copy-start(bf16[512,1536]{1,0:T(8,128)(2,1)} %param.20) | copy-start | bytes 4718596
Sparse Core Ops, SparseCore 0:
  106.4 60.9 all-gather.2
  170.1 59.9 all-gather.4
  239.9 67.0 reduce-scatter.5
  309.6 68.7 reduce-scatter.7
  382.6 88.6 reduce-scatter.3
where the time goes:
time: 492 us; the launch traced here: 491 us
  waiting for transfers between devices  331 us (67%)
  local copies, waits for them, and re-layouts  80.2 us (16%)
  matrix products  44.7 us (9%)
  between operations  14.8 us (3%)
  other arithmetic  14 us (3%)
  starting transfers between devices  6.05 us (1%)
    reduce_scatter x1, waiting for transfers between devices, local(): lax.psum_scatter(jnp.dot(hidden_all, outer_weight, preferred_element_type...  91.5 us
    reduce_scatter x1, waiting for transfers between devices, local(): lax.psum_scatter(term_outer.astype(jnp.bfloat16), 'lat', scatter_dimensio...  70 us
    gather x2, local copies, waits for them, and re-layouts, bias_matrix(): return bias_table[:, lookup]  61.1 us
    all_gather x1, waiting for transfers between devices, local(): cot_all = lax.all_gather(cot_coarse, 'lon', axis=0, tiled=True)  57.9 us
    reduce_scatter x1, waiting for transfers between devices, local(): lax.psum_scatter(term_inner.astype(jnp.bfloat16), 'lat', scatter_dimensio...  56.2 us
    all_gather x1, waiting for transfers between devices, local(): lifted_all = lax.all_gather(lifted, 'lon', axis=0, tiled=True)  55.3 us
  transfers between devices with their start and end apart: 7, of which 5 were waited for; matrix products, arithmetic and copies ran while one was open for 17% of the time, Pallas kernels for 0%

commit v1 on v0

--- a/solution.py
+++ b/solution.py
@@ -1,6 +1,8 @@
 import jax
 import jax.numpy as jnp
 from jax import lax
+from jax.experimental import pallas as pl
+from jax.experimental.pallas import tpu as pltpu
 from jax.sharding import PartitionSpec as P
 
 HEADS1 = 8
@@ -46,13 +48,16 @@
 
 
 def bias_matrix(bias_table, win_rows, win_cols):
-    places = jnp.arange(win_rows * win_cols, dtype=jnp.int32)
-    place_row = places // win_cols
-    place_col = places % win_cols
-    lookup = (place_row[:, None] - place_row[None, :] + win_rows - 1) * (2 * win_cols - 1) + (
-        place_col[:, None] - place_col[None, :] + win_cols - 1
-    )
-    return bias_table[:, lookup]
+    heads = bias_table.shape[0]
+    reach = 2 * win_cols - 1
+    flipped = bias_table[:, ::-1].reshape(heads, 2 * win_rows - 1, reach)
+    by_col = jnp.stack(
+        [flipped[:, :, win_cols - 1 - j : 2 * win_cols - 1 - j] for j in range(win_cols)], axis=1
+    )
+    by_row = jnp.stack(
+        [by_col[:, :, win_rows - 1 - i : 2 * win_rows - 1 - i] for i in range(win_rows)], axis=1
+    )
+    return by_row.reshape(heads, win_rows * win_cols, win_rows * win_cols)
 
 
 def window_attention(normed, qkv_weight, position_bias, win_rows, win_cols, head_count):
@@ -97,6 +102,300 @@
     grid_rows, grid_cols, total_width = grid.shape
     spread_out = grid.reshape(grid_rows, grid_cols, 2, 2, feat_width).transpose(0, 2, 1, 3, 4)
     return spread_out.reshape(grid_rows * 2, grid_cols * 2, feat_width)
+
+
+MESH = pl.DeviceIdType.MESH
+CELLS = 128
+HALF = 64
+
+
+class Copies:
+    def __init__(self, send_sems, recv_sems):
+        self.send_sems, self.recv_sems, self.started = send_sems, recv_sems, {}
+
+    def describe(self, name, src, dst, device):
+        return pltpu.make_async_remote_copy(
+            src_ref=src,
+            dst_ref=dst,
+            send_sem=self.send_sems.at[name],
+            recv_sem=self.recv_sems.at[name],
+            device_id=device,
+            device_id_type=MESH,
+        )
+
+    def start(self, name, src, dst, device):
+        copy = self.describe(name, src, dst, device)
+        copy.start()
+        self.started[name] = copy
+
+    def arrived(self, name, dst, device):
+        self.describe(name, dst, dst, device).wait_recv()
+
+    def finish(self):
+        for copy in self.started.values():
+            copy.wait_send()
+
+
+def exchange_kernel(
+    lifted_ref, cot_ref, inner_ref, outer_ref, eye_ref,
+    update_ref, grad_inner_ref, grad_outer_ref,
+    lift, cots, part, core_in, half_in, full_in, pair_in,
+    hidden_t, cot_pre_t, terms, ring_half, ring_full, side_out, side_in,
+    send_sems, recv_sems,
+):
+    lon, lat = lax.axis_index("lon"), lax.axis_index("lat")
+    core, y_hi, x = lon % 2, (lon // 2) % 2, lon // 4
+    z, y_lo = lat // 2, lat % 2
+    partner = {"lon": lon + 1 - 2 * core}
+    across = {"lon": lon + 2 - 4 * y_hi}
+    right, left = {"lon": (lon + 4) % 16}, {"lon": (lon + 12) % 16}
+    up, down = {"lat": (lat + 2) % 16}, {"lat": (lat + 14) % 16}
+    side = {"lat": lat + 1 - 2 * y_lo}
+
+    barrier = pltpu.get_barrier_semaphore()
+    neighbours = (partner, across, right, left, up, down, side)
+    for device in neighbours:
+        pl.semaphore_signal(barrier, inc=1, device_id=device, device_id_type=MESH)
+    pl.semaphore_wait(barrier, len(neighbours))
+
+    copies = Copies(send_sems, recv_sems)
+
+    def chip(dx, dy):
+        return ((x + dx) % 4) * 2 + (y_hi + dy) % 2
+
+    def at(array, dx, dy, dk=0):
+        return array.at[chip(dx, dy), (core + dk) % 2]
+
+    gathers = ((0, cots, cot_ref), (20, lift, lifted_ref))
+    for base, array, own in gathers:
+        array[chip(0, 0), core] = own[...]
+        for k, device in enumerate((partner, right, left, across)):
+            copies.start(base + k, at(array, 0, 0), at(array, 0, 0), device)
+
+    low, high = pl.ds(0, HALF), pl.ds(HALF, HALF)
+    hops = ((0, (1, 2), (7, 8, 9, 10, 11)), (1, (5, 6), (12, 13, 14, 15, 16)))
+
+    def process(dx, dy):
+        p = chip(dx, dy)
+        lifted = lift[p].reshape(2 * CELLS, -1)
+        cot = cots[p].reshape(2 * CELLS, -1)
+        pre = jnp.dot(lifted, inner_ref[...], preferred_element_type=jnp.float32)
+        value, slope = gelu_pair(pre)
+        hidden = value.astype(jnp.bfloat16)
+        update = jnp.dot(hidden, outer_ref[...], preferred_element_type=jnp.float32)
+        part[p] = update.astype(jnp.bfloat16).reshape(2, CELLS, -1)
+        cot_hidden = lax.dot_general(
+            cot, outer_ref[...], (((1,), (1,)), ((), ())), preferred_element_type=jnp.float32
+        )
+        cot_pre = (cot_hidden * slope).astype(jnp.bfloat16)
+        columns = pl.ds(pl.multiple_of(p * 2 * CELLS, 2 * CELLS), 2 * CELLS)
+        turn = (((1,), (1,)), ((), ()))
+        hidden_t[:, columns] = lax.dot_general(
+            eye_ref[...], hidden, turn, preferred_element_type=jnp.float32
+        ).astype(jnp.bfloat16)
+        cot_pre_t[:, columns] = lax.dot_general(
+            eye_ref[...], cot_pre, turn, preferred_element_type=jnp.float32
+        ).astype(jnp.bfloat16)
+        name = 40 + 4 * dy + dx
+        copies.start(name, part.at[p, 1 - core], core_in.at[p], partner)
+
+    def first_hop(base, array, dy, names, forward):
+        copies.arrived(base + names[0], at(array, 3, dy), right)
+        copies.start(
+            base + forward[0], at(array, 3, dy).at[low], at(array, 3, dy).at[low], right
+        )
+        copies.start(base + forward[1], at(array, 3, dy), at(array, 3, dy), partner)
+        copies.arrived(base + names[1], at(array, 1, dy), left)
+        copies.start(
+            base + forward[2], at(array, 1, dy).at[high], at(array, 1, dy).at[high], left
+        )
+        copies.start(base + forward[3], at(array, 1, dy), at(array, 1, dy), partner)
+
+    def across_hop(base, array):
+        copies.arrived(base + 3, at(array, 0, 1), across)
+        for k, device in ((5, right), (6, left), (4, partner)):
+            copies.start(base + k, at(array, 0, 1), at(array, 0, 1), device)
+
+    def second_hop(base, array, dy, forward):
+        copies.arrived(base + forward[0], at(array, 2, dy).at[low], right)
+        copies.arrived(base + forward[2], at(array, 2, dy).at[high], left)
+        copies.start(base + forward[4], at(array, 2, dy), at(array, 2, dy), partner)
+
+    def from_partner(base, array, dx, dy, name):
+        copies.arrived(base + name, at(array, dx, dy, 1), partner)
+
+    def both(step, *args):
+        for base, array, own in gathers:
+            step(base, array, *args)
+
+    both(first_hop, 0, *hops[0][1:])
+    both(across_hop)
+    both(from_partner, 0, 0, 0)
+    process(0, 0)
+    both(second_hop, 0, hops[0][2])
+    both(from_partner, 3, 0, 8)
+    process(3, 0)
+    both(from_partner, 1, 0, 10)
+    process(1, 0)
+    both(first_hop, 1, *hops[1][1:])
+    both(from_partner, 0, 1, 4)
+    process(0, 1)
+    both(from_partner, 2, 0, 11)
+    process(2, 0)
+    both(from_partner, 3, 1, 13)
+    process(3, 1)
+    both(from_partner, 1, 1, 15)
+    process(1, 1)
+    both(second_hop, 1, hops[1][2])
+    both(from_partner, 2, 1, 16)
+    process(2, 1)
+
+    def cores(dx, dy):
+        p = chip(dx, dy)
+        copies.arrived(40 + 4 * dy + dx, core_in.at[p], partner)
+        part[p, core] = (
+            part[p, core].astype(jnp.float32) + core_in[p].astype(jnp.float32)
+        ).astype(jnp.bfloat16)
+
+    def x_start(dy):
+        base = 48 + 4 * dy
+        cores(2, dy)
+        far = at(part, 2, dy)
+        copies.start(base, far.at[low], half_in.at[dy, 0], right)
+        copies.start(base + 1, far.at[high], half_in.at[dy, 1], left)
+        cores(1, dy)
+        cores(3, dy)
+        cores(0, dy)
+
+    def x_next(dy):
+        base = 48 + 4 * dy
+        copies.arrived(base, half_in.at[dy, 0], right)
+        p = chip(1, dy)
+        part[p, core, low, :] = (
+            part[p, core, low, :].astype(jnp.float32) + half_in[dy, 0].astype(jnp.float32)
+        ).astype(jnp.bfloat16)
+        copies.start(base + 2, part.at[p, core], full_in.at[dy, 0], right)
+        copies.arrived(base + 1, half_in.at[dy, 1], left)
+        p = chip(3, dy)
+        part[p, core, high, :] = (
+            part[p, core, high, :].astype(jnp.float32) + half_in[dy, 1].astype(jnp.float32)
+        ).astype(jnp.bfloat16)
+        copies.start(base + 3, part.at[p, core], full_in.at[dy, 1], left)
+
+    def x_last(dy):
+        base = 48 + 4 * dy
+        copies.arrived(base + 2, full_in.at[dy, 0], right)
+        copies.arrived(base + 3, full_in.at[dy, 1], left)
+        return (
+            part[chip(0, dy), core].astype(jnp.float32)
+            + full_in[dy, 0].astype(jnp.float32)
+            + full_in[dy, 1].astype(jnp.float32)
+        )
+
+    def zed(dz):
+        return (z + dz) % 8
+
+    def ring(step):
+        base = 56 + 2 * step
+        if step == 0:
+            far = terms.at[zed(4)]
+            copies.start(base, far.at[0], ring_half.at[0], up)
+            copies.start(base + 1, far.at[1], ring_half.at[1], down)
+            return
+        for way, device, mine in ((0, up, zed(4 - step)), (1, down, zed(4 + step))):
+            if step == 1:
+                copies.arrived(base - 2 + way, ring_half.at[way], device)
+                terms[mine, way] = (
+                    terms[mine, way].astype(jnp.float32) + ring_half[way].astype(jnp.float32)
+                ).astype(jnp.bfloat16)
+            else:
+                copies.arrived(base - 2 + way, ring_full.at[step - 2, way], device)
+                terms[mine] = (
+                    terms[mine].astype(jnp.float32)
+                    + ring_full[step - 2, way].astype(jnp.float32)
+                ).astype(jnp.bfloat16)
+            copies.start(base + way, terms.at[mine], ring_full.at[step - 1, way], device)
+
+    def ring_end():
+        total = terms[z].astype(jnp.float32)
+        for way, device in ((0, up), (1, down)):
+            copies.arrived(62 + way, ring_full.at[2, way], device)
+            total = total + ring_full[2, way].astype(jnp.float32)
+        side_out[...] = jnp.stack([total[0].T, total[1].T]).reshape(2, 2, HALF, -1)
+        sending = side_in.at[1]
+        sending[...] = side_out[:, 1 - y_lo].astype(jnp.bfloat16)
+        copies.start(64, sending, side_in.at[0], side)
+
+    x_start(1)
+    for j in range(4):
+        lanes = pl.ds(j * 256, 256)
+        for kind, rows, array in ((0, cot_pre_t, lift), (1, hidden_t, cots)):
+            term = jnp.dot(
+                rows[...],
+                array[:, :, :, lanes].reshape(16 * CELLS, 256),
+                preferred_element_type=jnp.float32,
+            ).astype(jnp.bfloat16)
+            terms[2 * j, kind] = term[:, :CELLS]
+            terms[2 * j + 1, kind] = term[:, CELLS:]
+    ring(0)
+    x_next(1)
+    x_start(0)
+    ring(1)
+    side_total = x_last(1)
+    part[chip(0, 1), core] = side_total.astype(jnp.bfloat16)
+    copies.start(65, at(part, 0, 1), pair_in, across)
+    x_next(0)
+    ring(2)
+    ring(3)
+    ring_end()
+    total = x_last(0)
+    copies.arrived(65, pair_in, across)
+    update_ref[...] = (total + pair_in[...].astype(jnp.float32)).astype(jnp.bfloat16)
+    copies.arrived(64, side_in.at[0], side)
+    final = side_out[:, y_lo] + side_in[0].astype(jnp.float32)
+    grad_inner_ref[...] = final[0]
+    grad_outer_ref[...] = final[1]
+    copies.finish()
+
+
+def exchange(lifted, cot_coarse, inner, outer):
+    eye = jnp.eye(256, dtype=jnp.bfloat16)
+    vmem = pl.BlockSpec(memory_space=pltpu.VMEM)
+    wide = (8, 2, CELLS, 1024)
+    bf16, f32 = jnp.bfloat16, jnp.float32
+    update, grad_inner, grad_outer = pl.pallas_call(
+        exchange_kernel,
+        out_shape=(
+            jax.ShapeDtypeStruct((CELLS, 1024), bf16),
+            jax.ShapeDtypeStruct((HALF, 256), f32),
+            jax.ShapeDtypeStruct((HALF, 256), f32),
+        ),
+        in_specs=[vmem] * 5,
+        out_specs=(vmem,) * 3,
+        scratch_shapes=[
+            pltpu.VMEM(wide, bf16),
+            pltpu.VMEM(wide, bf16),
+            pltpu.VMEM(wide, bf16),
+            pltpu.VMEM((8, CELLS, 1024), bf16),
+            pltpu.VMEM((2, 2, HALF, 1024), bf16),
+            pltpu.VMEM((2, 2, CELLS, 1024), bf16),
+            pltpu.VMEM((CELLS, 1024), bf16),
+            pltpu.VMEM((256, 16 * CELLS), bf16),
+            pltpu.VMEM((256, 16 * CELLS), bf16),
+            pltpu.VMEM((8, 2, 256, 128), bf16),
+            pltpu.VMEM((2, 256, 128), bf16),
+            pltpu.VMEM((3, 2, 2, 256, 128), bf16),
+            pltpu.VMEM((2, 2, HALF, 256), f32),
+            pltpu.VMEM((2, 2, HALF, 256), bf16),
+            pltpu.SemaphoreType.DMA((66,)),
+            pltpu.SemaphoreType.DMA((66,)),
+        ],
+        compiler_params=pltpu.CompilerParams(
+            collective_id=0, has_side_effects=True, vmem_limit_bytes=48 * 1024 * 1024
+        ),
+        name="exchange",
+    )(lifted, cot_coarse, inner, outer, eye)
+    return update, grad_inner, grad_outer.T
 
 
 def local(
@@ -133,45 +432,18 @@
         merged.reshape(-1, 4 * feat_width), merge_weight, preferred_element_type=jnp.float32
     ).astype(jnp.bfloat16)
     lifted = layer_norm(coarse_cells.astype(jnp.float32), coarse_gain).astype(jnp.bfloat16)
-    lifted_all = lax.all_gather(lifted, "lon", axis=0, tiled=True)
-    pre_all = jnp.dot(lifted_all, inner_weight, preferred_element_type=jnp.float32)
-    value_all, slope_all = gelu_pair(pre_all)
-    hidden_all = value_all.astype(jnp.bfloat16)
-    update = lax.psum_scatter(
-        jnp.dot(hidden_all, outer_weight, preferred_element_type=jnp.float32).astype(jnp.bfloat16),
-        "lon",
-        scatter_dimension=0,
-        tiled=True,
-    ).astype(jnp.float32)
-    back_cells = (coarse_cells.astype(jnp.float32) + update).astype(jnp.bfloat16)
-    raised = jnp.dot(back_cells, expand_weight, preferred_element_type=jnp.float32).reshape(
-        tile_rows // 2, tile_cols // 2, 4 * feat_width
-    )
-    prediction = (level_one.astype(jnp.float32) + unfold_quads(raised, feat_width)).astype(
-        jnp.bfloat16
-    )
     cot_folded = fold_quads(cotangent).reshape(-1, 4 * feat_width)
     cot_coarse = lax.dot_general(
         cot_folded, expand_weight, (((1,), (1,)), ((), ())), preferred_element_type=jnp.float32
     ).astype(jnp.bfloat16)
-    cot_all = lax.all_gather(cot_coarse, "lon", axis=0, tiled=True)
-    cot_hidden = lax.dot_general(
-        cot_all, outer_weight, (((1,), (1,)), ((), ())), preferred_element_type=jnp.float32
-    )
-    cot_pre = (cot_hidden * slope_all).astype(jnp.bfloat16)
-    term_inner = lax.dot_general(
-        lifted_all, cot_pre, (((0,), (0,)), ((), ())), preferred_element_type=jnp.float32
-    )
-    term_outer = lax.dot_general(
-        hidden_all, cot_all, (((0,), (0,)), ((), ())), preferred_element_type=jnp.float32
-    )
-    grad_inner, grad_outer = (
-        lax.psum_scatter(
-            term_inner.astype(jnp.bfloat16), "lat", scatter_dimension=0, tiled=True
-        ).astype(jnp.float32),
-        lax.psum_scatter(
-            term_outer.astype(jnp.bfloat16), "lat", scatter_dimension=1, tiled=True
-        ).astype(jnp.float32),
+    update, grad_inner, grad_outer = exchange(lifted, cot_coarse, inner_weight, outer_weight)
+    update = update.astype(jnp.float32)
+    back_cells = (coarse_cells.astype(jnp.float32) + update).astype(jnp.bfloat16)
+    raised = jnp.dot(back_cells, expand_weight, preferred_element_type=jnp.float32).reshape(
+        tile_rows // 2, tile_cols // 2, 4 * feat_width
+    )
+    prediction = (level_one.astype(jnp.float32) + unfold_quads(raised, feat_width)).astype(
+        jnp.bfloat16
     )
     return (prediction, grad_inner, grad_outer)
 

time: 492 us -> 152 us (0.31)
  waiting for transfers between devices: 331 us -> 0.01 us
  Pallas kernels: 0 us -> 75.3 us
  local copies, waits for them, and re-layouts: 80.2 us -> 39.5 us
  matrix products: 44.7 us -> 17.6 us
  between operations: 14.8 us -> 1.67 us
    reduce_scatter x3 -> x0, waiting for transfers between devices: 218 us -> none  [the longest x1 91.5 us: local(): lax.psum_scatter(jnp.dot(hidden_all, outer_weight, preferred_element_type...]
    all_gather x2 -> x0, waiting for transfers between devices: 113 us -> none  [the longest x1 57.9 us: local(): cot_all = lax.all_gather(cot_coarse, 'lon', axis=0, tiled=True)]
    pallas_call x0 -> x1, Pallas kernels: none -> 75.3 us  [exchange(): pl.pallas_call(exchange_kernel, out_shape=(jax.ShapeDtypeStruct((CELLS, 1...]
    gather x2 -> x0, local copies, waits for them, and re-layouts: 61.1 us -> none  [bias_matrix(): return bias_table[:, lookup]]
    dot_general x4 -> x0, matrix products: 25.2 us -> none  [the longest x1 9.69 us: local(): lax.dot_general(lifted_all, cot_pre, (((0,), (0,)), ((), ())), preferred_...]
    unnamed x21 -> x50, local copies, waits for them, and re-layouts: 0.18 us -> 9.02 us
  transfers between devices with their start and end apart: 7 -> 2, of which waited for: 5 -> 0; matrix products, arithmetic and copies ran while one was open for 17% -> 12% of each run, Pallas kernels for 0% -> 0%
where the time goes in v1:
time: 152 us; the launch traced here: 151 us
  Pallas kernels  75.3 us (50%)
  local copies, waits for them, and re-layouts  39.5 us (26%)
  matrix products  17.6 us (12%)
  other arithmetic  11.5 us (8%)
  starting transfers between devices  5.36 us (4%)
  between operations  1.67 us (1%)
    pallas_call x1, Pallas kernels, exchange(): pl.pallas_call(exchange_kernel, out_shape=(jax.ShapeDtypeStruct((CELLS, 1...  75.3 us
    unnamed x50, local copies, waits for them, and re-layouts  9.02 us
    another operation x2, local copies, waits for them, and re-layouts, unfold_quads(): grid.reshape(grid_rows, grid_cols, 2, 2, feat_width)  5.9 us
    convert_element_type x3, local copies, waits for them, and re-layouts, local(): fold_quads(level_one).astype(jnp.float32)  5.4 us
    ppermute x1, starting transfers between devices, with_halo(): lax.ppermute(head, axis, [((i + 1) % count, i) for i in range(count)])  5.36 us
    add x2, local copies, waits for them, and re-layouts, window_attention(): jnp.einsum('nqhd,nkhd->nhqk', queries, key_rows, preferred_element_type=j...  4.33 us
    convert_element_type x1, local copies, waits for them, and re-layouts, window_attention(): jnp.dot(windows, qkv_weight, preferred_element_type=jnp.float32)  4.26 us
    dot_general x1, matrix products, local(): lax.dot_general(cot_folded, expand_weight, (((1,), (1,)), ((), ())), pref...  3.7 us
  transfers between devices with their start and end apart: 2, of which 0 were waited for; matrix products, arithmetic and copies ran while one was open for 12% of the time, Pallas kernels for 0%

profile of v1, /device:TPU:8, one launch (start us, length us, event | category | flops | bytes accessed | tf_op | source)
XLA Modules:
  0.0 150.9 jit_solution(1256426264684705214)
XLA Ops:
  1.5 1.3 fusion.12
  2.8 1.5 multiply_reduce_fusion.1
  4.3 1.4 multiply_convert_fusion.1
  6.5 5.4 %collective-permute-start.1 = (bf16[16,16,512]{2,1,0:T(8,128)(2,1)}, bf16[16,16,512]{2,1,0:T(8,128)(2,1)}, u32[]{:S(2)}, u32[]{:S(2)}) collective-permute-start(bf16[16,16,512]{2,1,0:T(8,128)(2,1)} %get-tuple-element.9), channel_id=1, source_target_pairs={{1,0},{2,1},{3,2},{4,3},{5,4},{6,5},{7,6},{8,7},{9,8},{10,9},{11,1... | collective-permute-start | bytes 786440 | tf_op jit(solution)/shard_map/ppermute | solution.py:26
  14.5 0.9 fusion.22
  15.4 0.9 fusion.21
  16.3 0.9 fusion.20
  17.2 0.9 fusion.19
  18.0 0.9 fusion.18
  19.7 0.9 fusion.16
  20.6 3.3 %add.67 = f32[8,128,128]{2,0,1:T(8,128)S(1)} reshape(f32[8,8,16,8,16]{4,3,0,2,1:T(8,128)} %fusion.16) | data formatting | bytes 1048576 | tf_op jit(solution)/shard_map/add | solution.py:79
  23.9 1.0 copy.30
  26.6 3.7 %convolution_convert_fusion.1.cot_ref = bf16[128,1024]{1,0:T(8,128)(2,1)S(1)} fusion(bf16[128,2048]{1,0:T(8,128)(2,1)S(1)} %reshape_reshape.6, bf16[1024,2048]{1,0:T(8,128)(2,1)} %param.28), kind=kOutput, calls=%fused_computation.15 | convolution fusion | flops 537001984 | bytes 4980736 | tf_op jit(solution)/shard_map/dot_general | solution.py:436
  30.3 1.6 %fusion.14 = bf16[16,48,512]{2,1,0:T(8,128)(2,1)S(1)} fusion(s32[]{:T(128)S(6)} %select_n.6, bf16[16,16,512]{2,1,0:T(8,128)(2,1)} %collective-permute-done, bf16[16,32,512]{2,1,0:T(8,128)(2,1)S(1)} %multiply_convert_fusion.1, bf16[16,16,512]{2,1,0:T(8,128)(2,1)} %collective-permute-done.1), kind=kLoop, calls=%fused_computation.32 | loop fusion | flops 2359296 | bytes 1835012 | tf_op jit(solution)/shard_map/concatenate | solution.py:22
  32.0 2.8 %convolution_convert_fusion = bf16[6,128,1536]{2,1,0:T(8,128)(2,1)} fusion(bf16[6,128,512]{2,1,0:T(8,128)(2,1)S(1)} %bitcast.167, bf16[512,1536]{1,0:T(8,128)(2,1)S(1)} %copy-done), kind=kOutput, calls=%fused_computation.1 | convolution fusion | flops 1209139200 | bytes 4718592 | tf_op jit(solution)/shard_map/dot_general | solution.py:71
  34.8 4.3 %copy.26 = bf16[6,128,1536]{1,2,0:T(8,128)(2,1)} copy(bf16[6,128,1536]{2,1,0:T(8,128)(2,1)} %convolution_convert_fusion) | data formatting | bytes 4718592 | tf_op jit(solution)/shard_map/convert_element_type | solution.py:71
  39.1 2.1 %fusion.15 = f32[6,8,128,128]{2,3,1,0:T(8,128)S(1)} fusion(bf16[6,128,3,8,64]{1,4,3,2,0:T(8,128)(2,1)} %bitcast.159), kind=kOutput, calls=%fused_computation.34 | convolution fusion | flops 100663296 | bytes 4718592 | tf_op jit(solution)/shard_map/nqhd,nkhd->nhqk/dot_general | solution.py:79
  41.2 1.0 fusion.51
  42.2 1.7 %fusion.7 = bf16[6,128,8,64]{1,3,2,0:T(8,128)(2,1)S(1)} fusion(f32[6,8,128,128]{2,3,1,0:T(8,128)S(1)} %get-tuple-element.12, f32[6,8,128]{2,1,0:T(8,128)S(1)} %get-tuple-element.11, bf16[6,128,3,8,64]{1,4,3,2,0:T(8,128)(2,1)} %bitcast.160), kind=kOutput, calls=%fused_computation.12 | convolution fusion | flops 102629376 | bytes 4743168 | tf_op jit(solution)/shard_map/nhqk,nkhd->nqhd/dot_general | solution.py:86
  44.0 1.7 %copy.32 = bf16[6,128,8,64]{3,2,1,0:T(8,128)(2,1)} copy(bf16[6,128,8,64]{1,3,2,0:T(8,128)(2,1)S(1)} %fusion.7) | data formatting | bytes 1572864 | tf_op jit(solution)/shard_map/convert_element_type | solution.py:88
  45.7 2.9 %reshape.101 = bf16[2,3,8,16,512]{4,3,2,1,0:T(8,128)(2,1)S(1)} reshape(bf16[6,128,8,64]{3,2,1,0:T(8,128)(2,1)} %copy.32) | data formatting | bytes 1572864 | tf_op jit(solution)/shard_map/reshape | solution.py:89
  48.7 2.5 %fusion.9 = f32[16,32,512]{2,1,0:T(8,128)} fusion(bf16[16,32,512]{2,1,0:T(8,128)(2,1)S(1)} %copy-done.5, bf16[512,512]{1,0:T(8,128)(2,1)} %param.22, bf16[16,48,512]{2,1,0:T(8,128)(2,1)S(1)} %bitcast.165, s32[]{:T(128)S(6)} %select_n.7, f32[512]{0:T(512)S(1)} %copy-done.8, f32[16,32]{1,0:T(8,128)S(1)} %convert_element_type.76), kind=kOutput, calls=%fused_computation.14 | convolution fusion | flops 270008320 | bytes 2631684 | tf_op jit(solution)/shard_map/dot_general | solution.py:428
  51.2 1.8 %reshape.107 = f32[8,2,16,2,512]{4,3,2,1,0:T(2,128)S(1)} reshape(f32[16,32,512]{2,1,0:T(8,128)} %fusion.9) | data formatting | bytes 2097152 | tf_op jit(solution)/shard_map/convert_element_type | solution.py:430
  53.4 1.4 copy.49
  55.8 2.1 %reshape.105 = f32[128,2048]{1,0:T(8,128)S(1)} reshape(f32[8,16,2,2,512]{4,3,2,1,0:T(2,128)} %bitcast.161) | data formatting | bytes 2097152 | tf_op jit(solution)/shard_map/convert_element_type | solution.py:430
  58.0 3.2 %fusion.52 = (f32[128]{0:T(128)S(1)}, f32[128,1024]{1,0:T(8,128)S(1)}) fusion(bf16[2048,1024]{1,0:T(8,128)(2,1)} %param.24, f32[128,2048]{1,0:T(8,128)S(1)} %reshape.105, f32[2048]{0:T(1024)S(1)} %copy-done.10, f32[128]{0:T(128)S(1)} %rsqrt.29, f32[128]{0:T(128)S(1)} %div.33), kind=kOutput, calls=%fused_computation.108 | convolution fusion | flops 538312576 | bytes 5776896 | tf_op jit(solution)/shard_map/dot_general | solution.py:431
  61.6 75.3 %exchange.1 = (bf16[128,1024]{1,0:T(8,128)(2,1)S(1)}, f32[64,256]{1,0:T(8,128)S(1)}, f32[64,256]{1,0:T(8,128)S(1)}) custom-call(bf16[128,1024]{1,0:T(8,128)(2,1)S(1)} %multiply_convert_fusion.3.lifted_ref, bf16[128,1024]{1,0:T(8,128)(2,1)S(1)} %convolution_convert_fusion.1.cot_ref, bf16[1024,256]{1,0:T(8,128)(2,1)S(1)} %copy-done.1, ...), custom_call_target="tpu_custom_call" | custom-call | tf_op jit(solution)/shard_map/exchange/pallas_call | solution.py:366
  136.9 1.7 %fusion.29 = f32[128,2048]{1,0:T(8,128)} fusion(bf16[1024,2048]{1,0:T(8,128)(2,1)S(1)} %copy-done.3, f32[128,1024]{1,0:T(8,128)S(1)} %get-tuple-element.14, bf16[128,1024]{1,0:T(8,128)(2,1)S(1)} %get-tuple-element.6), kind=kOutput, calls=%fused_computation.62 | convolution fusion | flops 537264128 | bytes 6029312 | tf_op jit(solution)/shard_map/dot_general | solution.py:442
  138.6 3.2 %reshape_reshape.7 = f32[8,16,2,2,512]{4,3,2,1,0:T(2,128)} reshape(f32[128,2048]{1,0:T(8,128)} %fusion.29) | data formatting | bytes 2097152 | tf_op jit(solution)/shard_map/reshape;reshape | solution.py:103
  141.9 2.7 %copy.48 = f32[8,16,2,2,512]{4,3,1,2,0:T(2,128)} copy(f32[8,16,2,2,512]{4,3,2,1,0:T(2,128)} %reshape_reshape.7) | data formatting | bytes 2097152 | tf_op jit(solution)/shard_map/reshape;reshape | solution.py:103
  144.5 3.0 %reshape.104 = f32[16,32,512]{2,1,0:T(8,128)} reshape(f32[8,2,16,2,512]{4,3,2,1,0:T(2,128)} %bitcast.162) | data formatting | bytes 2097152 | tf_op jit(solution)/shard_map/reshape | solution.py:104
  147.5 2.2 %add_convert_fusion = bf16[16,32,512]{2,1,0:T(8,128)(2,1)} fusion(f32[16,32,512]{2,1,0:T(8,128)S(1)} %copy-done.4, f32[16,32,512]{2,1,0:T(8,128)} %reshape.104), kind=kLoop, calls=%fused_computation.23 | loop fusion | flops 524288 | bytes 2621440 | tf_op jit(solution)/shard_map/convert_element_type | solution.py:445
  (70 shorter events, 9.3 us)
Async XLA Ops:
  0.6 31.4 %copy-start = (bf16[512,1536]{1,0:T(8,128)(2,1)S(1)}, bf16[512,1536]{1,0:T(8,128)(2,1)}, u32[]{:S(2)}) copy-start(bf16[512,1536]{1,0:T(8,128)(2,1)} %param.20) | copy-start | bytes 4718596
  0.6 11.3 %copy-start.9 = (f32[8,465]{1,0:T(8,128)S(1)}, f32[8,465]{1,0:T(8,128)}, u32[]{:S(2)}) copy-start(f32[8,465]{1,0:T(8,128)} %param.21) | copy-start | bytes 44644
  6.5 23.8 %collective-permute-start = (bf16[16,16,512]{2,1,0:T(8,128)(2,1)}, bf16[16,16,512]{2,1,0:T(8,128)(2,1)}, u32[]{:S(2)}, u32[]{:S(2)}) collective-permute-start(bf16[16,16,512]{2,1,0:T(8,128)(2,1)} %get-tuple-element.10), channel_id=1, source_target_pairs={{0,1},{1,2},{2,3},{3,4},{4,5},{5,6},{6,7},{7,8},{8,9},{9,10},{10,1... | collective-permute-start | bytes 786440 | tf_op jit(solution)/shard_map/ppermute | solution.py:24
  6.5 23.8 %collective-permute-start.1 = (bf16[16,16,512]{2,1,0:T(8,128)(2,1)}, bf16[16,16,512]{2,1,0:T(8,128)(2,1)}, u32[]{:S(2)}, u32[]{:S(2)}) collective-permute-start(bf16[16,16,512]{2,1,0:T(8,128)(2,1)} %get-tuple-element.9), channel_id=1, source_target_pairs={{1,0},{2,1},{3,2},{4,3},{5,4},{6,5},{7,6},{8,7},{9,8},{10,9},{11,1... | collective-permute-start | bytes 786440 | tf_op jit(solution)/shard_map/ppermute | solution.py:26
  20.6 5.0 %copy-start.7 = (bf16[16,32,512]{2,1,0:T(8,128)(2,1)S(1)}, bf16[16,32,512]{2,1,0:T(8,128)(2,1)}, u32[]{:S(2)}) copy-start(bf16[16,32,512]{2,1,0:T(8,128)(2,1)} %param.29) | copy-start | bytes 1572868
  39.1 2.1 %copy-start.6 = (f32[8,128,128]{1,2,0:T(8,128)S(1)}, f32[8,128,128]{1,2,0:T(8,128)}, u32[]{:S(2)}) copy-start(f32[8,128,128]{1,2,0:T(8,128)} %copy.30) | copy-start | bytes 1572868
  43.9 4.7 %copy-start.5 = (bf16[16,32,512]{2,1,0:T(8,128)(2,1)S(1)}, bf16[16,32,512]{2,1,0:T(8,128)(2,1)}, u32[]{:S(2)}) copy-start(bf16[16,32,512]{2,1,0:T(8,128)(2,1)} %param.15) | copy-start | bytes 1572868
  43.9 4.7 %copy-start.8 = (f32[512]{0:T(512)S(1)}, f32[512]{0:T(512)}, u32[]{:S(2)}) copy-start(f32[512]{0:T(512)} %param.17) | copy-start | bytes 6148
  53.0 5.0 %copy-start.10 = (f32[2048]{0:T(1024)S(1)}, f32[2048]{0:T(1024)}, u32[]{:S(2)}) copy-start(f32[2048]{0:T(1024)} %param.23) | copy-start | bytes 24580
  58.0 3.5 %copy-start.11 = (f32[1024]{0:T(1024)S(1)}, f32[1024]{0:T(1024)}, u32[]{:S(2)}) copy-start(f32[1024]{0:T(1024)} %param.25) | copy-start | bytes 12292
  58.0 3.6 %copy-start.1 = (bf16[1024,256]{1,0:T(8,128)(2,1)S(1)}, bf16[1024,256]{1,0:T(8,128)(2,1)}, u32[]{:S(2)}) copy-start(bf16[1024,256]{1,0:T(8,128)(2,1)} %inner_ref.1) | copy-start | bytes 1572868
  58.0 3.6 %copy-start.2 = (bf16[256,1024]{1,0:T(8,128)(2,1)S(1)}, bf16[256,1024]{1,0:T(8,128)(2,1)}, u32[]{:S(2)}) copy-start(bf16[256,1024]{1,0:T(8,128)(2,1)} %outer_ref.1) | copy-start | bytes 1572868
  58.0 78.9 %copy-start.3 = (bf16[1024,2048]{1,0:T(8,128)(2,1)S(1)}, bf16[1024,2048]{1,0:T(8,128)(2,1)}, u32[]{:S(2)}) copy-start(bf16[1024,2048]{1,0:T(8,128)(2,1)} %param.28) | copy-start | bytes 12582916
  138.6 8.9 %copy-start.4 = (f32[16,32,512]{2,1,0:T(8,128)S(1)}, f32[16,32,512]{2,1,0:T(8,128)}, u32[]{:S(2)}) copy-start(f32[16,32,512]{2,1,0:T(8,128)} %fusion.9) | copy-start | bytes 3145732

commit v2 on v0

v2 whole, which is shorter than its diff:
```python
import jax
import jax.numpy as jnp
from jax import lax
from jax.experimental import pallas as pl
from jax.experimental.pallas import tpu as pltpu
from jax.sharding import PartitionSpec as P

HEADS1 = 8
WH = 8
WL = 16
D1 = 512
D2 = 1024
ROWS = 16
COLS = 32
CELLS = 128
HALF = 64
QUART = 32
COPIES = 84

NORM_EPS = 1e-05
GELU_SCALE = 0.7978845608028654
MESH = pl.DeviceIdType.MESH
BF16 = jnp.bfloat16
F32 = jnp.float32
LAST = (((1,), (1,)), ((), ()))


def normalise(values):
    centre = jnp.mean(values, axis=-1, keepdims=True)
    centred = values - centre
    spread = jnp.mean(centred * centred, axis=-1, keepdims=True)
    return centred * lax.rsqrt(spread + NORM_EPS)


def gelu_pair(pre_act):
    square = pre_act * pre_act
    inner = GELU_SCALE * (pre_act + 0.044715 * square * pre_act)
    tangent = jnp.tanh(inner)
    half = 0.5 * (1.0 + tangent)
    value = pre_act * half
    slope = half + value * (1.0 - tangent) * (GELU_SCALE + (3.0 * 0.044715 * GELU_SCALE) * square)
    return (value, slope)


def matmul(a, b):
    return jnp.dot(a, b, preferred_element_type=F32)


def matmul_t(a, b):
    return lax.dot_general(a, b, LAST, preferred_element_type=F32)


class Copies:
    def __init__(self, send_sems, recv_sems):
        self.send_sems, self.recv_sems = send_sems, recv_sems
        self.places, self.started = {}, []

    def describe(self, name, src, dst, device):
        place = self.places.setdefault(name, len(self.places))
        return pltpu.make_async_remote_copy(
            src_ref=src,
            dst_ref=dst,
            send_sem=self.send_sems.at[place],
            recv_sem=self.recv_sems.at[place],
            device_id=device,
            device_id_type=MESH,
        )

    def start(self, name, src, dst, device):
        copy = self.describe(name, src, dst, device)
        copy.start()
        self.started.append(copy)

    def arrived(self, name, dst, device):
        self.describe(name, dst, dst, device).wait_recv()

    def finish(self):
        for copy in self.started:
            copy.wait_send()


def window_kernel(
    shift_ref, features_ref, mask_ref, embed_ref, fine_gain_ref, bias_rows_ref, merge_gain_ref,
    coarse_gain_ref, cotangent_ref, eye_ref,
    qkv_hbm, mix_hbm, merge_hbm, inner_hbm, outer_hbm, expand_hbm,
    prediction_ref, grad_inner_ref, grad_outer_ref,
    qkv_ref, mix_ref, merge_ref, inner_ref, outer_ref, expand_ref,
    base, normed, halo, wide, bias, window, projected, attended, shifted, level, merged, coarse, back,
    lift, cots, part, core_in, across_in, half_in, full_in, pair_in,
    hidden_t, cot_pre_t, terms, ring_half, ring_full, side_out, side_in,
    load_sems, send_sems, recv_sems,
):
    lon, lat = lax.axis_index("lon"), lax.axis_index("lat")
    core, y_hi, x = lon % 2, (lon // 2) % 2, lon // 4
    z, y_lo = lat // 2, lat % 2
    east, west = {"lon": (lon + 1) % 16}, {"lon": (lon + 15) % 16}
    partner = {"lon": lon + 1 - 2 * core}
    across = {"lon": lon + 2 - 4 * y_hi}
    right, left = {"lon": (lon + 4) % 16}, {"lon": (lon + 12) % 16}
    up, down = {"lat": (lat + 2) % 16}, {"lat": (lat + 14) % 16}
    side = {"lat": lat + 1 - 2 * y_lo}

    loads = {}
    for k, (name, src, dst) in enumerate(
        (
            ("expand", expand_hbm, expand_ref),
            ("qkv", qkv_hbm, qkv_ref),
            ("mix", mix_hbm, mix_ref),
            ("merge", merge_hbm, merge_ref),
            ("inner", inner_hbm, inner_ref),
            ("outer", outer_hbm, outer_ref),
        )
    ):
        loads[name] = pltpu.make_async_copy(src, dst, load_sems.at[k])
        loads[name].start()

    barrier = pltpu.get_barrier_semaphore()
    neighbours = (east, west, partner, across, right, left, up, down, side)
    for device in neighbours:
        pl.semaphore_signal(barrier, inc=1, device_id=device, device_id_type=MESH)

    diagonal = lax.broadcasted_iota(jnp.int32, (COLS, COLS), 0) == lax.broadcasted_iota(
        jnp.int32, (COLS, COLS), 1
    )

    @pl.loop(0, ROWS, unroll=2)
    def _(r):
        land = mask_ref[pl.ds(r, 1), :].astype(F32)
        land = jnp.sum(jnp.where(diagonal, land, 0.0), axis=1, keepdims=True)
        cells = features_ref[r].astype(F32) + land * embed_ref[...]
        base[r] = cells
        rounded = (normalise(cells) * fine_gain_ref[...]).astype(BF16)
        normed[r] = rounded
        wide[r, WL : WL + COLS, :] = rounded.astype(F32)

    pl.semaphore_wait(barrier, len(neighbours))
    copies = Copies(send_sems, recv_sems)
    copies.start("halo e", normed.at[:, pl.ds(COLS - WL, WL), :], halo.at[0], east)
    copies.start("halo w", normed.at[:, pl.ds(0, WL), :], halo.at[1], west)

    def chip(dx, dy):
        return ((x + dx) % 4) * 2 + (y_hi + dy) % 2

    def fold(store):
        @pl.loop(0, ROWS // 2)
        def _(r):
            store(
                r,
                [
                    jnp.concatenate(
                        [level[r, i, c, pl.ds(j, COLS // 2, stride=2), :] for c in range(4)], axis=1
                    )
                    for i in range(2)
                    for j in range(2)
                ],
            )

    @pl.loop(0, ROWS // 2)
    def _(r):
        for i in range(2):
            cells = cotangent_ref[2 * r + i].astype(F32)
            for c in range(4):
                level[r, i, c] = cells[:, c * 128 : (c + 1) * 128]

    def store_cot(r, quads):
        rows = pl.ds(pl.multiple_of(r * 16, 16), 16)
        for q in range(4):
            merged[rows, q * D1 : (q + 1) * D1] = quads[q].astype(BF16)

    fold(store_cot)
    loads["expand"].wait()

    @pl.loop(0, 4)
    def _(j):
        lanes = pl.ds(pl.multiple_of(j * 256, 256), 256)
        cots[chip(0, 0), core, :, lanes] = matmul_t(merged[...], expand_ref[lanes, :]).astype(BF16)

    low, high = pl.ds(0, HALF), pl.ds(HALF, HALF)
    first, second = pl.ds(0, QUART), pl.ds(QUART, QUART)

    class Gather:
        def __init__(self, name, array):
            self.name, self.array = name, array

        def at(self, dx, dy, rows=None, dk=0):
            block = self.array.at[chip(dx, dy), (core + dk) % 2]
            return block if rows is None else block.at[rows]

        def send(self, name, dx, dy, rows, device):
            block = self.at(dx, dy, rows)
            copies.start(self.name + name, block, block, device)

        def came(self, name, dx, dy, rows, device):
            copies.arrived(self.name + name, self.at(dx, dy, rows), device)

        def share(self, dx, dy):
            self.send("p%d%d" % (dx, dy), dx, dy, None, partner)

        def begin(self):
            self.send("yl", 0, 0, low, across)
            self.send("xr", 0, 0, None, right)
            self.send("xl", 0, 0, None, left)
            self.send("y0", 0, 0, high, across)
            self.share(0, 0)

        def near(self):
            self.came("xr", 3, 0, None, right)
            self.send("fr", 3, 0, low, right)
            self.send("y3", 3, 0, high, across)
            self.came("xl", 1, 0, None, left)
            self.send("fl", 1, 0, high, left)
            self.send("y1", 1, 0, high, across)
            self.share(3, 0)
            self.share(1, 0)

        def other(self):
            self.came("yl", 0, 1, low, across)
            self.send("or", 0, 1, low, right)
            self.send("ol", 0, 1, low, left)

        def far(self):
            self.came("fl", 2, 0, high, left)
            self.send("y2", 2, 0, high, across)
            self.came("fr", 2, 0, low, right)
            self.share(2, 0)

        def other_near(self):
            self.came("or", 3, 1, low, right)
            self.send("gr", 3, 1, first, right)
            self.came("ol", 1, 1, low, left)
            self.send("gl", 1, 1, second, left)
            self.came("y0", 0, 1, high, across)
            self.share(0, 1)
            self.came("y3", 3, 1, high, across)
            self.share(3, 1)
            self.came("y1", 1, 1, high, across)
            self.share(1, 1)

        def other_far(self):
            self.came("gr", 2, 1, first, right)
            self.came("gl", 2, 1, second, left)
            self.came("y2", 2, 1, high, across)
            self.share(2, 1)

        def shared(self, dx, dy):
            copies.arrived(self.name + "p%d%d" % (dx, dy), self.at(dx, dy, None, 1), partner)

    gather_cot, gather_lift = Gather("c", cots), Gather("l", lift)
    gather_cot.begin()

    lane = lax.broadcasted_iota(jnp.int32, (WL, 128), 1)

    @pl.loop(0, HEADS1)
    def _(h):
        halves = []
        for k in range(2):
            total = jnp.zeros((WL, 128), F32)
            for i in range(8 if k == 0 else 7):
                row = jnp.broadcast_to(bias_rows_ref[h, 8 * k + i : 8 * k + i + 1, :], (WL, 128))
                turned = pltpu.roll(row, (128 - 15 + 16 * i) % 128, 1, stride=1, stride_axis=0)
                total = jnp.where(lane // 16 == i, turned, total)
            halves.append(total)
        both = jnp.concatenate(halves, axis=1)
        for i in range(WH):
            start = (WH - 1 - i) * WL
            bias[h, i * WL : (i + 1) * WL, :] = both[:, start : start + 128]

    offset = shift_ref[0]
    first_head = lax.broadcasted_iota(jnp.int32, (CELLS, 128), 1) < 64
    ones = jnp.ones((CELLS, 128), BF16)

    def attend(w):
        @pl.loop(0, ROWS, unroll=2)
        def _(r):
            cells = wide[r, w * WL : (w + 2) * WL, :]
            window[r] = pltpu.roll(cells, 2 * WL - offset, 0)[:WL].astype(BF16)

        @pl.loop(0, 6)
        def _(j):
            lanes = pl.ds(pl.multiple_of(j * 256, 256), 256)
            rows = window[...].reshape(ROWS * WL, D1)
            projected[:, lanes] = matmul(rows, qkv_ref[:, lanes]).astype(BF16)

        @pl.loop(0, 8, unroll=2)
        def _(k):
            band, pair = k // 4, k % 4
            rows = pl.ds(pl.multiple_of(band * CELLS, CELLS), CELLS)

            def lanes(kind):
                return pl.ds(pl.multiple_of(kind * D1 + pair * 128, 128), 128)

            queries = projected[rows, lanes(0)]
            zero = jnp.zeros_like(queries)
            queries = jnp.concatenate(
                [jnp.where(first_head, queries, zero), jnp.where(first_head, zero, queries)], axis=0
            )
            scores = matmul_t(queries, projected[rows, lanes(1)]) * 0.125
            scores = scores + bias[pl.ds(2 * pair, 2)].reshape(2 * CELLS, 128)
            expo = jnp.exp(scores - jnp.max(scores, axis=1, keepdims=True)).astype(BF16)
            values = jnp.concatenate([projected[rows, lanes(2)], ones], axis=1)
            sums = matmul(expo, values)
            heads = sums[:, :128] / sums[:, 128:]
            heads = jnp.where(first_head, heads[:CELLS], heads[CELLS:])
            attended[pl.ds(band * WH, WH), w * WL : (w + 1) * WL, lanes(0)] = heads.reshape(
                WH, WL, 128
            )

    loads["qkv"].wait()
    attend(1)
    gather_cot.near()
    copies.arrived("halo e", halo.at[0], east)
    copies.arrived("halo w", halo.at[1], west)

    @pl.loop(0, ROWS)
    def _(r):
        wide[r, 0:WL, :] = halo[0, r].astype(F32)
        wide[r, WL + COLS :, :] = halo[1, r].astype(F32)

    attend(0)
    gather_cot.other()
    attend(2)
    gather_cot.far()

    loads["mix"].wait()

    @pl.loop(0, ROWS, unroll=2)
    def _(r):
        shifted[r] = pltpu.roll(attended[r], COLS + offset, 0)[:COLS].astype(BF16)

    @pl.loop(0, 4)
    def _(i):
        rows = pl.ds(i * 4, 4)
        mixed = matmul(shifted[rows].reshape(CELLS, D1), mix_ref[...]).reshape(4, COLS, D1)
        mixed = (base[rows] + mixed).astype(BF16).astype(F32).reshape(2, 2, COLS, D1)
        for c in range(4):
            level[pl.ds(i * 2, 2), :, c] = mixed[..., c * 128 : (c + 1) * 128]

    def store_merged(r, quads):
        centre = sum(jnp.sum(quad, axis=1, keepdims=True) for quad in quads) / (4 * D1)
        quads = [quad - centre for quad in quads]
        spread = sum(jnp.sum(quad * quad, axis=1, keepdims=True) for quad in quads) / (4 * D1)
        scale = lax.rsqrt(spread + NORM_EPS)
        rows = pl.ds(pl.multiple_of(r * 16, 16), 16)
        for q in range(4):
            lanes = slice(q * D1, (q + 1) * D1)
            merged[rows, lanes] = (quads[q] * scale * merge_gain_ref[:, lanes]).astype(BF16)

    fold(store_merged)
    loads["merge"].wait()

    @pl.loop(0, 4)
    def _(j):
        lanes = pl.ds(pl.multiple_of(j * 256, 256), 256)
        coarse[:, lanes] = matmul(merged[...], merge_ref[:, lanes]).astype(BF16)

    @pl.loop(0, 4)
    def _(i):
        rows = pl.ds(pl.multiple_of(i * 32, 32), 32)
        lift[chip(0, 0), core, rows, :] = (
            normalise(coarse[rows, :].astype(F32)) * coarse_gain_ref[...]
        ).astype(BF16)

    gather_lift.begin()
    gather_cot.other_near()
    loads["inner"].wait()
    loads["outer"].wait()

    def process(dx, dy):
        gather_cot.shared(dx, dy)
        gather_lift.shared(dx, dy)
        p = chip(dx, dy)
        pre = matmul(lift[p].reshape(2 * CELLS, D2), inner_ref[...])
        value, slope = gelu_pair(pre)
        hidden = value.astype(BF16)
        part[p] = matmul(hidden, outer_ref[...]).astype(BF16).reshape(2, CELLS, D2)
        copies.start("s%d%d" % (dx, dy), part.at[p, 1 - core], core_in.at[p], partner)
        cot_hidden = matmul_t(cots[p].reshape(2 * CELLS, D2), outer_ref[...])
        cot_pre = (cot_hidden * slope).astype(BF16)
        columns = pl.ds(pl.multiple_of(p * 2 * CELLS, 2 * CELLS), 2 * CELLS)
        hidden_t[:, columns] = matmul_t(eye_ref[...], hidden).astype(BF16)
        cot_pre_t[:, columns] = matmul_t(eye_ref[...], cot_pre).astype(BF16)

    process(0, 0)
    gather_lift.near()
    gather_cot.other_far()
    gather_lift.other()
    process(3, 0)
    process(1, 0)
    gather_lift.far()
    process(2, 0)
    gather_lift.other_near()
    process(0, 1)
    process(3, 1)
    process(1, 1)
    gather_lift.other_far()
    process(2, 1)

    def add_to(place, rows, *others):
        total = part[place, core, rows, :].astype(F32)
        for other in others:
            total = total + other.astype(F32)
        part[place, core, rows, :] = total.astype(BF16)

    def cores(dx, dy):
        p = chip(dx, dy)
        copies.arrived("s%d%d" % (dx, dy), core_in.at[p], partner)
        add_to(p, slice(None), core_in[p])
        if dy == 1:
            block = part.at[p, core, high]
            copies.start("t%d" % dx, block, across_in.at[dx], across)

    def from_across(dx):
        copies.arrived("t%d" % dx, across_in.at[dx], across)
        add_to(chip(dx, 0), high, across_in[dx])

    class Chain:
        def __init__(self, name, place, dy, start):
            self.name, self.place, self.dy = name, place, dy
            self.rows = pl.ds(start, HALF)
            self.firsts, self.seconds = pl.ds(start, QUART), pl.ds(start + QUART, QUART)

        def begin(self):
            block = part.at[chip(2, self.dy), core]
            here = half_in.at[self.place]
            copies.start(self.name + "0", block.at[self.firsts], here.at[0], right)
            copies.start(self.name + "1", block.at[self.seconds], here.at[1], left)

        def next(self):
            here, there = half_in.at[self.place], full_in.at[self.place]
            for way, device, dx, rows in (
                (0, right, 1, self.firsts),
                (1, left, 3, self.seconds),
            ):
                copies.arrived(self.name + "%d" % way, here.at[way], device)
                p = chip(dx, self.dy)
                add_to(p, rows, here[way])
                copies.start(
                    self.name + "%d" % (2 + way),
                    part.at[p, core, self.rows],
                    there.at[way],
                    device,
                )

        def end(self):
            there = full_in.at[self.place]
            copies.arrived(self.name + "2", there.at[0], right)
            copies.arrived(self.name + "3", there.at[1], left)
            return (
                part[chip(0, self.dy), core, self.rows, :].astype(F32)
                + there[0].astype(F32)
                + there[1].astype(F32)
            )

    away, here_low, here_high = Chain("a", 0, 1, 0), Chain("b", 1, 0, 0), Chain("d", 2, 0, HALF)

    def zed(dz):
        return (z + dz) % 8

    def ring(step):
        if step == 0:
            distant = terms.at[zed(4)]
            copies.start("z00", distant.at[0], ring_half.at[0], up)
            copies.start("z01", distant.at[1], ring_half.at[1], down)
            return
        for way, device, mine in ((0, up, zed(4 - step)), (1, down, zed(4 + step))):
            name = "z%d%d" % (step - 1, way)
            if step == 1:
                copies.arrived(name, ring_half.at[way], device)
                terms[mine, way] = (
                    terms[mine, way].astype(F32) + ring_half[way].astype(F32)
                ).astype(BF16)
            else:
                copies.arrived(name, ring_full.at[step - 2, way], device)
                terms[mine] = (
                    terms[mine].astype(F32) + ring_full[step - 2, way].astype(F32)
                ).astype(BF16)
            copies.start("z%d%d" % (step, way), terms.at[mine], ring_full.at[step - 1, way], device)

    def ring_end():
        total = terms[z].astype(F32)
        for way, device in ((0, up), (1, down)):
            copies.arrived("z3%d" % way, ring_full.at[2, way], device)
            total = total + ring_full[2, way].astype(F32)
        for kind in range(2):
            side_out[kind] = total[kind].T.reshape(2, HALF, 256)
        side_in[1] = side_out[:, 1 - y_lo].astype(BF16)
        copies.start("side", side_in.at[1], side_in.at[0], side)

    cores(2, 1)
    away.begin()
    cores(1, 1)
    cores(3, 1)
    cores(0, 1)
    cores(2, 0)
    here_low.begin()

    @pl.loop(0, 4)
    def _(j):
        lanes = pl.ds(pl.multiple_of(j * 256, 256), 256)
        for kind, rows, array in ((0, cot_pre_t, lift), (1, hidden_t, cots)):
            term = matmul(rows[...], array[:, :, :, lanes].reshape(16 * CELLS, 256)).astype(BF16)
            terms[2 * j, kind] = term[:, :128]
            terms[2 * j + 1, kind] = term[:, 128:]

    ring(0)
    away.next()
    cores(1, 0)
    cores(3, 0)
    here_low.next()
    from_across(2)
    here_high.begin()
    ring(1)
    part[chip(0, 1), core, low, :] = away.end().astype(BF16)
    copies.start("pair", part.at[chip(0, 1), core, low], pair_in, across)
    ring(2)
    from_across(1)
    from_across(3)
    here_high.next()
    cores(0, 0)
    ring(3)
    loads_done = here_low.end()
    from_across(0)
    copies.arrived("pair", pair_in, across)
    back[low, :] = (
        coarse[low, :].astype(F32) + loads_done + pair_in[...].astype(F32)
    ).astype(BF16)
    ring_end()
    back[high, :] = (coarse[high, :].astype(F32) + here_high.end()).astype(BF16)

    for q in range(4):
        raised = matmul(back[...], expand_ref[:, q * D1 : (q + 1) * D1])
        cells = pl.ds(q % 2, COLS // 2, stride=2)
        for c in range(4):
            block = raised[:, c * 128 : (c + 1) * 128].reshape(ROWS // 2, COLS // 2, 128)
            level[:, q // 2, c, cells, :] = level[:, q // 2, c, cells, :] + block

    @pl.loop(0, ROWS // 2)
    def _(r):
        for i in range(2):
            for c in range(4):
                prediction_ref[2 * r + i, :, c * 128 : (c + 1) * 128] = level[r, i, c].astype(BF16)

    copies.arrived("side", side_in.at[0], side)
    final = side_out[:, y_lo] + side_in[0].astype(F32)
    grad_inner_ref[...] = final[0]
    grad_outer_ref[...] = final[1].T
    copies.finish()


def local(
    features, land_mask, land_embed, window_shift, fine_gain, qkv_weight, bias_table, mix_weight,
    merge_gain, merge_weight, coarse_gain, inner_weight, outer_weight, expand_weight, cotangent,
):
    vmem = pl.BlockSpec(memory_space=pltpu.VMEM)
    smem = pl.BlockSpec(memory_space=pltpu.SMEM)
    anywhere = pl.BlockSpec(memory_space=pl.ANY)
    reach = 2 * WL - 1
    bias_rows = jnp.pad(
        bias_table[:, ::-1].reshape(HEADS1, 2 * WH - 1, reach), ((0, 0), (0, 1), (0, 128 - reach))
    )
    wide_block = pltpu.VMEM((8, 2, CELLS, D2), BF16)
    return pl.pallas_call(
        window_kernel,
        out_shape=(
            jax.ShapeDtypeStruct((ROWS, COLS, D1), BF16),
            jax.ShapeDtypeStruct((HALF, 256), F32),
            jax.ShapeDtypeStruct((256, HALF), F32),
        ),
        in_specs=[smem] + [vmem] * 9 + [anywhere] * 6,
        out_specs=(vmem,) * 3,
        scratch_shapes=[
            pltpu.VMEM((D1, 3 * D1), BF16),
            pltpu.VMEM((D1, D1), BF16),
            pltpu.VMEM((4 * D1, D2), BF16),
            pltpu.VMEM((D2, 256), BF16),
            pltpu.VMEM((256, D2), BF16),
            pltpu.VMEM((D2, 4 * D1), BF16),
            pltpu.VMEM((ROWS, COLS, D1), F32),
            pltpu.VMEM((ROWS, COLS, D1), BF16),
            pltpu.VMEM((2, ROWS, WL, D1), BF16),
            pltpu.VMEM((ROWS, COLS + 2 * WL, D1), F32),
            pltpu.VMEM((HEADS1, CELLS, CELLS), F32),
            pltpu.VMEM((ROWS, WL, D1), BF16),
            pltpu.VMEM((ROWS * WL, 3 * D1), BF16),
            pltpu.VMEM((ROWS, COLS + WL, D1), F32),
            pltpu.VMEM((ROWS, COLS, D1), BF16),
            pltpu.VMEM((ROWS // 2, 2, 4, COLS, 128), F32),
            pltpu.VMEM((CELLS, 4 * D1), BF16),
            pltpu.VMEM((CELLS, D2), BF16),
            pltpu.VMEM((CELLS, D2), BF16),
            wide_block,
            wide_block,
            wide_block,
            pltpu.VMEM((8, CELLS, D2), BF16),
            pltpu.VMEM((4, HALF, D2), BF16),
            pltpu.VMEM((3, 2, QUART, D2), BF16),
            pltpu.VMEM((3, 2, HALF, D2), BF16),
            pltpu.VMEM((HALF, D2), BF16),
            pltpu.VMEM((256, 16 * CELLS), BF16),
            pltpu.VMEM((256, 16 * CELLS), BF16),
            pltpu.VMEM((8, 2, 256, 128), BF16),
            pltpu.VMEM((2, 256, 128), BF16),
            pltpu.VMEM((3, 2, 2, 256, 128), BF16),
            pltpu.VMEM((2, 2, HALF, 256), F32),
            pltpu.VMEM((2, 2, HALF, 256), BF16),
            pltpu.SemaphoreType.DMA((6,)),
            pltpu.SemaphoreType.DMA((COPIES,)),
            pltpu.SemaphoreType.DMA((COPIES,)),
        ],
        compiler_params=pltpu.CompilerParams(
            collective_id=0, has_side_effects=True, vmem_limit_bytes=56 * 1024 * 1024
        ),
        name="window",
    )(
        window_shift, features, land_mask, land_embed[None], fine_gain[None], bias_rows,
        merge_gain[None], coarse_gain[None], cotangent, jnp.eye(256, dtype=BF16),
        qkv_weight, mix_weight, merge_weight, inner_weight, outer_weight, expand_weight,
    )


def solution(mesh):
    return jax.shard_map(
        local,
        mesh=mesh,
        in_specs=(
            P("lat", "lon", None),
            P("lat", "lon"),
            P(),
            P(),
            P(),
            P(),
            P(),
            P(),
            P(),
            P(),
            P(),
            P(None, "lon"),
            P("lon", None),
            P(),
            P("lat", "lon", None),
        ),
        out_specs=(P("lat", "lon", None), P("lat", "lon"), P("lon", "lat")),
        check_vma=False,
    )
```

time: 492 us -> 94.2 us (0.19)
  waiting for transfers between devices: 331 us -> 0 us
  Pallas kernels: 0 us -> 84.1 us
  local copies, waits for them, and re-layouts: 80.2 us -> 7.36 us
  matrix products: 44.7 us -> 0 us
  between operations: 14.8 us -> 1.3 us
  other arithmetic: 14 us -> 0.67 us
  starting transfers between devices: 6.05 us -> 0 us
    reduce_scatter x3 -> x0, waiting for transfers between devices: 218 us -> none  [the longest x1 91.5 us: local(): lax.psum_scatter(jnp.dot(hidden_all, outer_weight, preferred_element_type...]
    all_gather x2 -> x0, waiting for transfers between devices: 113 us -> none  [the longest x1 57.9 us: local(): cot_all = lax.all_gather(cot_coarse, 'lon', axis=0, tiled=True)]
    pallas_call x0 -> x1, Pallas kernels: none -> 84.1 us  [local(): pl.pallas_call(window_kernel, out_shape=(jax.ShapeDtypeStruct((ROWS, COLS...]
    gather x2 -> x0, local copies, waits for them, and re-layouts: 61.1 us -> none  [bias_matrix(): return bias_table[:, lookup]]
    dot_general x11 -> x0, matrix products: 44.7 us -> none  [the longest x1 9.69 us: local(): lax.dot_general(lifted_all, cot_pre, (((0,), (0,)), ((), ())), preferred_...]
    convert_element_type x5 -> x0, local copies, waits for them, and re-layouts: 9.34 us -> none  [the longest x1 4.26 us: window_attention(): jnp.dot(windows, qkv_weight, preferred_element_type=jnp.float32)]
    convert_element_type x6 -> x1, other arithmetic: 7.97 us -> 0.67 us  [local(): jnp.eye(256, dtype=BF16)]
    ppermute x2 -> x0, starting transfers between devices: 5.36 us -> none  [the longest x1 5.36 us: with_halo(): lax.ppermute(head, axis, [((i + 1) % count, i) for i in range(count)])]
  transfers between devices with their start and end apart: 7 -> 0, of which waited for: 5 -> 0; matrix products, arithmetic and copies ran while one was open for 17% -> 0% of each run, Pallas kernels for 0% -> 0%
where the time goes in v2:
time: 94.2 us; the launch traced here: 93.5 us
  Pallas kernels  84.1 us (89%)
  local copies, waits for them, and re-layouts  7.36 us (8%)
  between operations  1.3 us (1%)
    pallas_call x1, Pallas kernels, local(): pl.pallas_call(window_kernel, out_shape=(jax.ShapeDtypeStruct((ROWS, COLS...  84.1 us
    unnamed x4, local copies, waits for them, and re-layouts  5.01 us

profile of v2, /device:TPU:8, one launch (start us, length us, event | category | flops | bytes accessed | tf_op | source)
XLA Modules:
  0.0 93.5 jit_solution(16031896902661691249)
XLA Ops:
  1.3 1.6 %reverse = f32[8,512]{1,0:T(8,128)S(1)} reverse(f32[8,512]{1,0:T(8,128)} %bitcast.5), dimensions={1} | reverse | bytes 32768
  2.9 0.1 slice
  2.9 0.1 reshape.9
  3.0 0.6 pad.4.bias_rows_ref
  3.7 0.7 fusion.eye_ref
  4.3 84.1 %window.1 = (bf16[16,32,512]{2,1,0:T(8,128)(2,1)}, f32[64,256]{1,0:T(8,128)}, f32[256,64]{1,0:T(8,128)}) custom-call(s32[1]{0:T(128)S(6)} %copy.22.shift_ref, bf16[16,32,512]{2,1,0:T(8,128)(2,1)} %features_ref.1, s32[16,32]{1,0:T(8,128)} %mask_ref.1, f32[1,512]{1,0:T(1,128)} %bitcast.8, f32[1,512]{1,0:T(1,128)} %bitcast.9, f32[8,16,128]{2,1,0:T(8,128)} %pad.4.bias_rows_ref, ...), custom_call_target="tpu_custom_call" | custom-call | tf_op jit(solution)/shard_map/window/pallas_call | solution.py:562
  88.5 1.6 %copy.19 = f32[256,64]{0,1:T(8,128)} copy(f32[256,64]{1,0:T(8,128)} %get-tuple-element.8) | data formatting | bytes 131072 | tf_op jit(solution)/shard_map/window/pallas_call | solution.py:562
  90.1 1.9 %copy.23 = bf16[16,32,512]{2,1,0:T(8,128)(2,1)} copy(bf16[16,32,512]{2,1,0:T(8,128)(2,1)} %get-tuple-element.12) | data formatting | bytes 1048576
  92.0 1.5 %copy.24 = f32[64,256]{1,0:T(8,128)} copy(f32[64,256]{1,0:T(8,128)} %get-tuple-element.13) | data formatting | bytes 131072

commit v3 on v2

v3 whole, which is shorter than its diff:
```python
import jax
import jax.numpy as jnp
from jax import lax
from jax.experimental import pallas as pl
from jax.experimental.pallas import tpu as pltpu
from jax.sharding import PartitionSpec as P

HEADS1 = 8
WH = 8
WL = 16
D1 = 512
D2 = 1024
ROWS = 16
COLS = 32
CELLS = 128
HALF = 64
QUART = 32
COPIES = 96

NORM_EPS = 1e-05
GELU_SCALE = 0.7978845608028654
MESH = pl.DeviceIdType.MESH
BF16 = jnp.bfloat16
F32 = jnp.float32
LAST = (((1,), (1,)), ((), ()))


def normalise(values):
    centre = jnp.mean(values, axis=-1, keepdims=True)
    centred = values - centre
    spread = jnp.mean(centred * centred, axis=-1, keepdims=True)
    return centred * lax.rsqrt(spread + NORM_EPS)


def gelu_pair(pre_act):
    square = pre_act * pre_act
    inner = GELU_SCALE * (pre_act + 0.044715 * square * pre_act)
    tangent = jnp.tanh(inner)
    half = 0.5 * (1.0 + tangent)
    value = pre_act * half
    slope = half + value * (1.0 - tangent) * (GELU_SCALE + (3.0 * 0.044715 * GELU_SCALE) * square)
    return (value, slope)


def matmul(a, b):
    return jnp.dot(a, b, preferred_element_type=F32)


def matmul_t(a, b):
    return lax.dot_general(a, b, LAST, preferred_element_type=F32)


class Copies:
    def __init__(self, send_sems, recv_sems):
        self.send_sems, self.recv_sems = send_sems, recv_sems
        self.places, self.started = {}, []

    def describe(self, name, src, dst, device):
        place = self.places.setdefault(name, len(self.places))
        return pltpu.make_async_remote_copy(
            src_ref=src,
            dst_ref=dst,
            send_sem=self.send_sems.at[place],
            recv_sem=self.recv_sems.at[place],
            device_id=device,
            device_id_type=MESH,
        )

    def start(self, name, src, dst, device):
        copy = self.describe(name, src, dst, device)
        copy.start()
        self.started.append(copy)

    def arrived(self, name, dst, device):
        self.describe(name, dst, dst, device).wait_recv()

    def finish(self):
        for copy in self.started:
            copy.wait_send()


def window_kernel(
    shift_ref, features_ref, mask_ref, embed_ref, fine_gain_ref, table_ref, merge_gain_ref,
    coarse_gain_ref, cotangent_ref,
    qkv_hbm, mix_hbm, merge_hbm, inner_hbm, outer_hbm, expand_hbm,
    prediction_ref, grad_inner_ref, grad_outer_ref,
    qkv_ref, mix_ref, merge_ref, inner_ref, outer_ref, expand_ref,
    padded, table_rows, base, normed, halo, wide, bias, window, projected, attended, shifted, level, merged, coarse, back,
    lift, cots, part, core_in, across_in, half_in, full_in, pair_in,
    hidden_t, cot_pre_t, sums, terms, ring_in, side_out, side_in,
    load_sems, send_sems, recv_sems,
):
    lon, lat = lax.axis_index("lon"), lax.axis_index("lat")
    core, y_hi, x = lon % 2, (lon // 2) % 2, lon // 4
    z, y_lo = lat // 2, lat % 2
    east, west = {"lon": (lon + 1) % 16}, {"lon": (lon + 15) % 16}
    partner = {"lon": lon + 1 - 2 * core}
    across = {"lon": lon + 2 - 4 * y_hi}
    right, left = {"lon": (lon + 4) % 16}, {"lon": (lon + 12) % 16}
    up, down = {"lat": (lat + 2) % 16}, {"lat": (lat + 14) % 16}
    side = {"lat": lat + 1 - 2 * y_lo}

    loads = {}
    for k, (name, src, dst) in enumerate(
        (
            ("expand", expand_hbm, expand_ref),
            ("qkv", qkv_hbm, qkv_ref),
            ("mix", mix_hbm, mix_ref),
            ("merge", merge_hbm, merge_ref),
            ("inner", inner_hbm, inner_ref),
            ("outer", outer_hbm, outer_ref),
        )
    ):
        loads[name] = pltpu.make_async_copy(src, dst, load_sems.at[k])
        loads[name].start()

    barrier = pltpu.get_barrier_semaphore()
    neighbours = (east, west, partner, across, right, left, up, down, side)
    for device in neighbours:
        pl.semaphore_signal(barrier, inc=1, device_id=device, device_id_type=MESH)

    diagonal = lax.broadcasted_iota(jnp.int32, (COLS, COLS), 0) == lax.broadcasted_iota(
        jnp.int32, (COLS, COLS), 1
    )

    @pl.loop(0, ROWS, unroll=2)
    def _(r):
        land = mask_ref[pl.ds(r, 1), :].astype(F32)
        land = jnp.sum(jnp.where(diagonal, land, 0.0), axis=1, keepdims=True)
        cells = features_ref[r].astype(F32) + land * embed_ref[...]
        base[r] = cells
        rounded = (normalise(cells) * fine_gain_ref[...]).astype(BF16)
        normed[r] = rounded
        wide[r, WL : WL + COLS, :] = rounded.astype(F32)

    pl.semaphore_wait(barrier, len(neighbours))
    copies = Copies(send_sems, recv_sems)
    copies.start("halo e", normed.at[:, pl.ds(COLS - WL, WL), :], halo.at[0], east)
    copies.start("halo w", normed.at[:, pl.ds(0, WL), :], halo.at[1], west)

    padded[...] = jnp.zeros_like(padded)
    padded[:, 0 : table_ref.shape[1]] = table_ref[...]
    offsets = padded[...]
    top = offsets.astype(BF16)
    rest = offsets - top.astype(F32)
    middle = rest.astype(BF16)
    bottom = (rest - middle.astype(F32)).astype(BF16)
    turn = lax.broadcasted_iota(jnp.int32, (512, 640), 0) + lax.broadcasted_iota(
        jnp.int32, (512, 640), 1
    )
    turn = jnp.where(turn == table_ref.shape[1] - 1, 1.0, 0.0).astype(BF16)
    flipped = matmul(top, turn) + matmul(middle, turn) + matmul(bottom, turn)
    for i in range(2 * WH - 1):
        start = i * (2 * WL - 1)
        table_rows[i] = flipped[:, start : start + 128]
    lane = lax.broadcasted_iota(jnp.int32, (WL, 128), 1)

    @pl.loop(0, HEADS1)
    def _(h):
        halves = []
        for k in range(2):
            total = jnp.zeros((WL, 128), F32)
            for i in range(8 if k == 0 else 7):
                row = jnp.broadcast_to(table_rows[8 * k + i, pl.ds(h, 1), :], (WL, 128))
                turned = pltpu.roll(row, (128 - 15 + 16 * i) % 128, 1, stride=1, stride_axis=0)
                total = jnp.where(lane // 16 == i, turned, total)
            halves.append(total)
        both = jnp.concatenate(halves, axis=1)
        for i in range(WH):
            start = (WH - 1 - i) * WL
            bias[h, i * WL : (i + 1) * WL, :] = both[:, start : start + 128]

    def place(dx, dy):
        return 4 * dy + (0, 1, 3, 2)[dx % 4]

    def fold(store):
        @pl.loop(0, ROWS // 2)
        def _(r):
            store(
                r,
                [
                    jnp.concatenate(
                        [level[r, i, c, pl.ds(j, COLS // 2, stride=2), :] for c in range(4)], axis=1
                    )
                    for i in range(2)
                    for j in range(2)
                ],
            )

    @pl.loop(0, ROWS // 2)
    def _(r):
        for i in range(2):
            cells = cotangent_ref[2 * r + i].astype(F32)
            for c in range(4):
                level[r, i, c] = cells[:, c * 128 : (c + 1) * 128]

    def store_cot(r, quads):
        rows = pl.ds(pl.multiple_of(r * 16, 16), 16)
        for q in range(4):
            merged[rows, q * D1 : (q + 1) * D1] = quads[q].astype(BF16)

    fold(store_cot)
    loads["expand"].wait()

    @pl.loop(0, 4)
    def _(j):
        lanes = pl.ds(pl.multiple_of(j * 256, 256), 256)
        cots[0, 0, :, lanes] = matmul_t(merged[...], expand_ref[lanes, :]).astype(BF16)

    low, high = pl.ds(0, 80), pl.ds(80, 48)
    front, rear = pl.ds(0, HALF), pl.ds(HALF, HALF)
    ahead, behind = pl.ds(0, 48), pl.ds(48, 32)
    moves = {"r": (right, -1, 0, 0), "l": (left, 1, 0, 0), "y": (across, 0, 1, 0), "p": (partner, 0, 0, 1)}

    class Gather:
        def __init__(self, name, array):
            self.name, self.array = name, array

        def at(self, dx, dy, rows=None, dk=0):
            block = self.array.at[place(dx, dy), dk]
            return block if rows is None else block.at[rows]

        def send(self, name, dx, dy, rows, way):
            device, mx, my, mk = moves[way]
            there = self.at(dx + mx, (dy + my) % 2, rows, mk)
            copies.start(self.name + name, self.at(dx, dy, rows), there, device)

        def came(self, name, dx, dy, rows, way):
            copies.arrived(self.name + name, self.at(dx, dy, rows), moves[way][0])

        def share(self, dx, dy):
            self.send("p%d%d" % (dx, dy), dx, dy, None, "p")

        def shared(self, dx, dy):
            copies.arrived(self.name + "p%d%d" % (dx, dy), self.at(dx, dy, None, 1), partner)

        def begin(self):
            self.send("yl", 0, 0, low, "y")
            self.send("r0", 0, 0, front, "r")
            self.send("l0", 0, 0, rear, "l")
            self.send("r1", 0, 0, rear, "r")
            self.send("l1", 0, 0, front, "l")
            self.send("y0", 0, 0, high, "y")
            self.share(0, 0)

        def near(self):
            self.came("r0", 3, 0, front, "r")
            self.send("fr", 3, 0, front, "r")
            self.came("l0", 1, 0, rear, "l")
            self.send("fl", 1, 0, rear, "l")
            self.send("y1", 1, 0, high, "y")

        def other(self):
            self.came("yl", 0, 1, low, "y")
            self.send("or0", 0, 1, ahead, "r")
            self.send("ol0", 0, 1, behind, "l")
            self.send("or1", 0, 1, behind, "r")
            self.send("ol1", 0, 1, ahead, "l")

        def near_rest(self):
            self.came("r1", 3, 0, rear, "r")
            self.send("y3", 3, 0, high, "y")
            self.share(3, 0)
            self.came("l1", 1, 0, front, "l")
            self.share(1, 0)

        def far(self):
            self.came("fl", 2, 0, rear, "l")
            self.send("y2", 2, 0, high, "y")
            self.came("fr", 2, 0, front, "r")
            self.share(2, 0)

        def other_near(self):
            self.came("or0", 3, 1, ahead, "r")
            self.send("gr", 3, 1, ahead, "r")
            self.came("ol0", 1, 1, behind, "l")
            self.send("gl", 1, 1, behind, "l")
            self.came("y0", 0, 1, high, "y")
            self.share(0, 1)

        def other_rest(self):
            self.came("or1", 3, 1, behind, "r")
            self.came("ol1", 1, 1, ahead, "l")
            self.came("y1", 1, 1, high, "y")
            self.share(1, 1)
            self.came("y3", 3, 1, high, "y")
            self.share(3, 1)

        def other_far(self):
            self.came("y2", 2, 1, high, "y")
            self.came("gr", 2, 1, ahead, "r")
            self.came("gl", 2, 1, behind, "l")
            self.share(2, 1)

    gather_cot, gather_lift = Gather("c", cots), Gather("l", lift)
    gather_cot.begin()

    offset = shift_ref[0]
    first_head = lax.broadcasted_iota(jnp.int32, (CELLS, 128), 1) < 64
    ones = jnp.ones((CELLS, 128), BF16)

    def attend(w):
        @pl.loop(0, ROWS, unroll=2)
        def _(r):
            cells = wide[r, w * WL : (w + 2) * WL, :]
            window[r] = pltpu.roll(cells, 2 * WL - offset, 0)[:WL].astype(BF16)

        @pl.loop(0, 6)
        def _(j):
            lanes = pl.ds(pl.multiple_of(j * 256, 256), 256)
            rows = window[...].reshape(ROWS * WL, D1)
            projected[:, lanes] = matmul(rows, qkv_ref[:, lanes]).astype(BF16)

        @pl.loop(0, 8, unroll=4)
        def _(k):
            band, pair = k // 4, k % 4
            rows = pl.ds(pl.multiple_of(band * CELLS, CELLS), CELLS)

            def lanes(kind):
                return pl.ds(pl.multiple_of(kind * D1 + pair * 128, 128), 128)

            queries = projected[rows, lanes(0)] * 0.125
            zero = jnp.zeros_like(queries)
            queries = jnp.concatenate(
                [jnp.where(first_head, queries, zero), jnp.where(first_head, zero, queries)], axis=0
            )
            scores = matmul_t(queries, projected[rows, lanes(1)])
            scores = scores + bias[pl.ds(2 * pair, 2)].reshape(2 * CELLS, 128)
            expo = jnp.exp(scores - jnp.max(scores, axis=1, keepdims=True)).astype(BF16)
            values = jnp.concatenate([projected[rows, lanes(2)], ones], axis=1)
            sums = matmul(expo, values)
            heads = sums[:, :128] / sums[:, 128:]
            heads = jnp.where(first_head, heads[:CELLS], heads[CELLS:])
            attended[pl.ds(band * WH, WH), w * WL : (w + 1) * WL, lanes(0)] = heads.reshape(
                WH, WL, 128
            )

    loads["qkv"].wait()
    attend(1)
    gather_cot.near()
    gather_cot.other()
    copies.arrived("halo e", halo.at[0], east)
    copies.arrived("halo w", halo.at[1], west)

    @pl.loop(0, ROWS)
    def _(r):
        wide[r, 0:WL, :] = halo[0, r].astype(F32)
        wide[r, WL + COLS :, :] = halo[1, r].astype(F32)

    attend(0)
    gather_cot.near_rest()
    attend(2)
    gather_cot.far()
    gather_cot.other_near()

    loads["mix"].wait()

    @pl.loop(0, ROWS, unroll=2)
    def _(r):
        shifted[r] = pltpu.roll(attended[r], COLS + offset, 0)[:COLS].astype(BF16)

    @pl.loop(0, 4)
    def _(i):
        rows = pl.ds(i * 4, 4)
        mixed = matmul(shifted[rows].reshape(CELLS, D1), mix_ref[...]).reshape(4, COLS, D1)
        mixed = (base[rows] + mixed).astype(BF16).astype(F32).reshape(2, 2, COLS, D1)
        for c in range(4):
            level[pl.ds(i * 2, 2), :, c] = mixed[..., c * 128 : (c + 1) * 128]

    def store_merged(r, quads):
        centre = sum(jnp.sum(quad, axis=1, keepdims=True) for quad in quads) / (4 * D1)
        quads = [quad - centre for quad in quads]
        spread = sum(jnp.sum(quad * quad, axis=1, keepdims=True) for quad in quads) / (4 * D1)
        scale = lax.rsqrt(spread + NORM_EPS)
        rows = pl.ds(pl.multiple_of(r * 16, 16), 16)
        for q in range(4):
            lanes = slice(q * D1, (q + 1) * D1)
            merged[rows, lanes] = (quads[q] * scale * merge_gain_ref[:, lanes]).astype(BF16)

    fold(store_merged)
    loads["merge"].wait()

    @pl.loop(0, 4)
    def _(j):
        lanes = pl.ds(pl.multiple_of(j * 256, 256), 256)
        coarse[:, lanes] = matmul(merged[...], merge_ref[:, lanes]).astype(BF16)

    @pl.loop(0, 4)
    def _(i):
        rows = pl.ds(pl.multiple_of(i * 32, 32), 32)
        lift[0, 0, rows, :] = (
            normalise(coarse[rows, :].astype(F32)) * coarse_gain_ref[...]
        ).astype(BF16)

    gather_lift.begin()
    gather_cot.other_rest()
    loads["inner"].wait()
    loads["outer"].wait()

    unit = lax.broadcasted_iota(jnp.int32, (256, 256), 0) == lax.broadcasted_iota(
        jnp.int32, (256, 256), 1
    )
    unit = jnp.where(unit, 1.0, 0.0).astype(BF16)

    def process(dx, dy):
        gather_cot.shared(dx, dy)
        gather_lift.shared(dx, dy)
        p = place(dx, dy)
        pre = matmul(lift[p].reshape(2 * CELLS, D2), inner_ref[...])
        value, slope = gelu_pair(pre)
        hidden = value.astype(BF16)
        part[p] = matmul(hidden, outer_ref[...]).astype(BF16).reshape(2, CELLS, D2)
        copies.start("s%d%d" % (dx, dy), part.at[p, 1], core_in.at[p], partner)
        cot_hidden = matmul_t(cots[p].reshape(2 * CELLS, D2), outer_ref[...])
        cot_pre = (cot_hidden * slope).astype(BF16)
        columns = slice(p * 2 * CELLS, (p + 1) * 2 * CELLS)
        hidden_t[:, columns] = matmul_t(unit, hidden).astype(BF16)
        cot_pre_t[:, columns] = matmul_t(unit, cot_pre).astype(BF16)

    def gradients(begin, end):
        @pl.loop(0, 4)
        def _(j):
            lanes = pl.ds(pl.multiple_of(j * 256, 256), 256)
            for kind, rows, array in ((0, cot_pre_t, lift), (1, hidden_t, cots)):
                cells = array[begin:end, :, :, lanes].reshape((end - begin) * 2 * CELLS, 256)
                term = matmul(rows[:, begin * 2 * CELLS : end * 2 * CELLS], cells)
                if begin > 0:
                    term = term + sums[kind, :, lanes]
                if end < 8:
                    sums[kind, :, lanes] = term
                else:
                    terms[2 * j, kind] = term[:, :128].astype(BF16)
                    terms[2 * j + 1, kind] = term[:, 128:].astype(BF16)

    lower, upper = pl.ds(0, HALF), pl.ds(HALF, HALF)

    def add_to(p, rows, *others):
        total = part[p, 0, rows, :].astype(F32)
        for other in others:
            total = total + other.astype(F32)
        part[p, 0, rows, :] = total.astype(BF16)

    def cores(dx, dy):
        p = place(dx, dy)
        copies.arrived("s%d%d" % (dx, dy), core_in.at[p], partner)
        add_to(p, slice(None), core_in[p])
        if dy == 1:
            copies.start("t%d" % dx, part.at[p, 0, upper], across_in.at[dx], across)

    def from_across(dx):
        copies.arrived("t%d" % dx, across_in.at[dx], across)
        add_to(place(dx, 0), upper, across_in[dx])

    class Chain:
        def __init__(self, name, number, dy, start):
            self.name, self.number, self.dy = name, number, dy
            self.rows = pl.ds(start, HALF)
            self.firsts, self.seconds = pl.ds(start, QUART), pl.ds(start + QUART, QUART)

        def begin(self):
            block = part.at[place(2, self.dy), 0]
            here = half_in.at[self.number]
            copies.start(self.name + "0", block.at[self.firsts], here.at[0], right)
            copies.start(self.name + "1", block.at[self.seconds], here.at[1], left)

        def next(self):
            here, there = half_in.at[self.number], full_in.at[self.number]
            for way, device, dx, rows in (
                (0, right, 1, self.firsts),
                (1, left, 3, self.seconds),
            ):
                copies.arrived(self.name + "%d" % way, here.at[way], device)
                p = place(dx, self.dy)
                add_to(p, rows, here[way])
                copies.start(
                    self.name + "%d" % (2 + way),
                    part.at[p, 0, self.rows],
                    there.at[way],
                    device,
                )

        def end(self):
            there = full_in.at[self.number]
            copies.arrived(self.name + "2", there.at[0], right)
            copies.arrived(self.name + "3", there.at[1], left)
            return (
                part[place(0, self.dy), 0, self.rows, :].astype(F32)
                + there[0].astype(F32)
                + there[1].astype(F32)
            )

    away, here_low, here_high = Chain("a", 0, 1, 0), Chain("b", 1, 0, 0), Chain("d", 2, 0, HALF)

    def zed(dz):
        return (z + dz) % 8

    ways = ((0, up, 1), (1, down, -1))

    def ring_send(step, way, kind):
        device, sign = ways[way][1:]
        mine = terms.at[zed(sign * (4 - step) + 8), kind]
        copies.start("z%d%d%d" % (step, way, kind), mine, ring_in.at[step, way, kind], device)

    def ring_begin():
        ring_send(0, 0, 0)
        ring_send(0, 1, 1)
        ring_send(1, 0, 1)
        ring_send(1, 1, 0)

    def ring_step(step, kind, both=True):
        for way, device, sign in ways:
            if not both and way != kind:
                continue
            here = ring_in.at[step - 1, way, kind]
            copies.arrived("z%d%d%d" % (step - 1, way, kind), here, device)
            mine = zed(sign * (4 - step) + 8)
            terms[mine, kind] = (terms[mine, kind].astype(F32) + here[...].astype(F32)).astype(BF16)
            ring_send(step, way, kind)

    def ring_end(kind):
        total = terms[z, kind].astype(F32)
        for way, device, sign in ways:
            here = ring_in.at[3, way, kind]
            copies.arrived("z3%d%d" % (way, kind), here, device)
            total = total + here[...].astype(F32)
        side_out[kind] = total.T.reshape(2, HALF, 256)
        side_in[1, kind] = side_out[kind, 1 - y_lo].astype(BF16)
        copies.start("side%d" % kind, side_in.at[1, kind], side_in.at[0, kind], side)

    process(0, 0)
    gather_lift.near()
    gather_cot.other_far()
    gather_lift.other()
    gather_lift.near_rest()
    process(3, 0)
    process(1, 0)
    gather_lift.far()
    cores(0, 0)
    cores(3, 0)
    cores(1, 0)
    gather_lift.other_near()
    process(2, 0)
    process(0, 1)
    cores(2, 0)
    here_low.begin()
    gradients(0, 4)
    gather_lift.other_rest()
    cores(0, 1)
    process(1, 1)
    process(3, 1)
    here_low.next()
    cores(1, 1)
    cores(3, 1)
    gradients(4, 7)
    gather_lift.other_far()
    process(2, 1)
    gradients(7, 8)
    ring_begin()
    cores(2, 1)
    away.begin()
    from_across(0)
    from_across(1)
    from_across(3)
    ring_step(1, 0, False)
    ring_step(1, 1, False)
    away.next()
    from_across(2)
    here_high.begin()
    ring_step(2, 0)
    ring_step(2, 1)
    near_total = here_low.end()
    part[place(0, 1), 0, lower, :] = away.end().astype(BF16)
    copies.start("pair", part.at[place(0, 1), 0, lower], pair_in, across)
    here_high.next()
    ring_step(3, 0)
    ring_step(3, 1)
    ring_end(0)
    copies.arrived("pair", pair_in, across)
    back[lower, :] = (
        coarse[lower, :].astype(F32) + near_total + pair_in[...].astype(F32)
    ).astype(BF16)
    back[upper, :] = (coarse[upper, :].astype(F32) + here_high.end()).astype(BF16)
    ring_end(1)

    for q in range(4):
        raised = matmul(back[...], expand_ref[:, q * D1 : (q + 1) * D1])
        cells = pl.ds(q % 2, COLS // 2, stride=2)
        for c in range(4):
            block = raised[:, c * 128 : (c + 1) * 128].reshape(ROWS // 2, COLS // 2, 128)
            level[:, q // 2, c, cells, :] = level[:, q // 2, c, cells, :] + block

    @pl.loop(0, ROWS // 2)
    def _(r):
        for i in range(2):
            for c in range(4):
                prediction_ref[2 * r + i, :, c * 128 : (c + 1) * 128] = level[r, i, c].astype(BF16)

    for kind, out in ((0, grad_inner_ref), (1, grad_outer_ref)):
        copies.arrived("side%d" % kind, side_in.at[0, kind], side)
        out[...] = side_out[kind, y_lo] + side_in[0, kind].astype(F32)
    copies.finish()


def local(
    features, land_mask, land_embed, window_shift, fine_gain, qkv_weight, bias_table, mix_weight,
    merge_gain, merge_weight, coarse_gain, inner_weight, outer_weight, expand_weight, cotangent,
):
    vmem = pl.BlockSpec(memory_space=pltpu.VMEM)
    smem = pl.BlockSpec(memory_space=pltpu.SMEM)
    anywhere = pl.BlockSpec(memory_space=pl.ANY)
    wide_block = pltpu.VMEM((8, 2, CELLS, D2), BF16)
    prediction, grad_inner, grad_outer = pl.pallas_call(
        window_kernel,
        out_shape=(
            jax.ShapeDtypeStruct((ROWS, COLS, D1), BF16),
            jax.ShapeDtypeStruct((HALF, 256), F32),
            jax.ShapeDtypeStruct((HALF, 256), F32),
        ),
        in_specs=[smem] + [vmem] * 8 + [anywhere] * 6,
        out_specs=(vmem,) * 3,
        scratch_shapes=[
            pltpu.VMEM((D1, 3 * D1), BF16),
            pltpu.VMEM((D1, D1), BF16),
            pltpu.VMEM((4 * D1, D2), BF16),
            pltpu.VMEM((D2, 256), BF16),
            pltpu.VMEM((256, D2), BF16),
            pltpu.VMEM((D2, 4 * D1), BF16),
            pltpu.VMEM((HEADS1, 512), F32),
            pltpu.VMEM((2 * WH - 1, HEADS1, 128), F32),
            pltpu.VMEM((ROWS, COLS, D1), F32),
            pltpu.VMEM((ROWS, COLS, D1), BF16),
            pltpu.VMEM((2, ROWS, WL, D1), BF16),
            pltpu.VMEM((ROWS, COLS + 2 * WL, D1), F32),
            pltpu.VMEM((HEADS1, CELLS, CELLS), F32),
            pltpu.VMEM((ROWS, WL, D1), BF16),
            pltpu.VMEM((ROWS * WL, 3 * D1), BF16),
            pltpu.VMEM((ROWS, COLS + WL, D1), F32),
            pltpu.VMEM((ROWS, COLS, D1), BF16),
            pltpu.VMEM((ROWS // 2, 2, 4, COLS, 128), F32),
            pltpu.VMEM((CELLS, 4 * D1), BF16),
            pltpu.VMEM((CELLS, D2), BF16),
            pltpu.VMEM((CELLS, D2), BF16),
            wide_block,
            wide_block,
            wide_block,
            pltpu.VMEM((8, CELLS, D2), BF16),
            pltpu.VMEM((4, HALF, D2), BF16),
            pltpu.VMEM((3, 2, QUART, D2), BF16),
            pltpu.VMEM((3, 2, HALF, D2), BF16),
            pltpu.VMEM((HALF, D2), BF16),
            pltpu.VMEM((256, 16 * CELLS), BF16),
            pltpu.VMEM((256, 16 * CELLS), BF16),
            pltpu.VMEM((2, 256, D2), F32),
            pltpu.VMEM((8, 2, 256, 128), BF16),
            pltpu.VMEM((4, 2, 2, 256, 128), BF16),
            pltpu.VMEM((2, 2, HALF, 256), F32),
            pltpu.VMEM((2, 2, HALF, 256), BF16),
            pltpu.SemaphoreType.DMA((6,)),
            pltpu.SemaphoreType.DMA((COPIES,)),
            pltpu.SemaphoreType.DMA((COPIES,)),
        ],
        compiler_params=pltpu.CompilerParams(
            collective_id=0, has_side_effects=True, vmem_limit_bytes=46 * 1024 * 1024
        ),
        name="window",
    )(
        window_shift, features, land_mask, land_embed[None], fine_gain[None], bias_table,
        merge_gain[None], coarse_gain[None], cotangent,
        qkv_weight, mix_weight, merge_weight, inner_weight, outer_weight, expand_weight,
    )
    return prediction, grad_inner, grad_outer.T


def solution(mesh):
    return jax.shard_map(
        local,
        mesh=mesh,
        in_specs=(
            P("lat", "lon", None),
            P("lat", "lon"),
            P(),
            P(),
            P(),
            P(),
            P(),
            P(),
            P(),
            P(),
            P(),
            P(None, "lon"),
            P("lon", None),
            P(),
            P("lat", "lon", None),
        ),
        out_specs=(P("lat", "lon", None), P("lat", "lon"), P("lon", "lat")),
        check_vma=False,
    )
```

time: 94.2 us -> 95.7 us (1.016)
  local copies, waits for them, and re-layouts: 7.36 us -> 12.8 us
  Pallas kernels: 84.1 us -> 81 us
    unnamed x4 -> x27, local copies, waits for them, and re-layouts: 5.01 us -> 12.8 us
    pallas_call x1, Pallas kernels: 84.1 us -> 81 us  [local(): pl.pallas_call(window_kernel, out_shape=(jax.ShapeDtypeStruct((ROWS, COLS...]
    pallas_call x1 -> x0, local copies, waits for them, and re-layouts: 1.62 us -> none  [local(): pl.pallas_call(window_kernel, out_shape=(jax.ShapeDtypeStruct((ROWS, COLS...]
where the time goes in v3:
time: 95.7 us; the launch traced here: 95.1 us
  Pallas kernels  81 us (85%)
  local copies, waits for them, and re-layouts  12.8 us (13%)
  between operations  1.31 us (1%)
    pallas_call x1, Pallas kernels, local(): pl.pallas_call(window_kernel, out_shape=(jax.ShapeDtypeStruct((ROWS, COLS...  81 us
    unnamed x27, local copies, waits for them, and re-layouts  12.8 us

profile of v3, /device:TPU:8, one launch (start us, length us, event | category | flops | bytes accessed | tf_op | source)
XLA Modules:
  0.0 95.1 jit_solution(16874648735431167237)
XLA Ops:
  1.3 0.0 copy-start
  1.3 1.4 %copy-done = bf16[512,1536]{1,0:T(8,128)(2,1)S(1)} copy-done((bf16[512,1536]{1,0:T(8,128)(2,1)S(1)}, bf16[512,1536]{1,0:T(8,128)(2,1)}, u32[]{:S(2)}) %copy-start) | copy-done | bytes 1572888
  2.7 0.0 copy-start.1
  2.7 1.0 %copy-done.1 = bf16[16,32,512]{2,1,0:T(8,128)(2,1)S(1)} copy-done((bf16[16,32,512]{2,1,0:T(8,128)(2,1)S(1)}, bf16[16,32,512]{2,1,0:T(8,128)(2,1)}, u32[]{:S(2)}) %copy-start.1) | copy-done | bytes 524312
  3.7 0.0 copy-start.2
  3.7 1.0 %copy-done.2 = bf16[16,32,512]{2,1,0:T(8,128)(2,1)S(1)} copy-done((bf16[16,32,512]{2,1,0:T(8,128)(2,1)S(1)}, bf16[16,32,512]{2,1,0:T(8,128)(2,1)}, u32[]{:S(2)}) %copy-start.2) | copy-done | bytes 524312
  4.8 0.0 copy-start.3
  4.8 1.0 %copy-done.3 = bf16[512,512]{1,0:T(8,128)(2,1)S(1)} copy-done((bf16[512,512]{1,0:T(8,128)(2,1)S(1)}, bf16[512,512]{1,0:T(8,128)(2,1)}, u32[]{:S(2)}) %copy-start.3) | copy-done | bytes 524312
  5.8 0.0 copy-start.4
  5.8 1.0 %copy-done.4 = bf16[1024,256]{1,0:T(8,128)(2,1)S(1)} copy-done((bf16[1024,256]{1,0:T(8,128)(2,1)S(1)}, bf16[1024,256]{1,0:T(8,128)(2,1)}, u32[]{:S(2)}) %copy-start.4) | copy-done | bytes 524312
  6.9 0.0 copy-start.5
  6.9 1.0 %copy-done.5 = bf16[256,1024]{1,0:T(8,128)(2,1)S(1)} copy-done((bf16[256,1024]{1,0:T(8,128)(2,1)S(1)}, bf16[256,1024]{1,0:T(8,128)(2,1)}, u32[]{:S(2)}) %copy-start.5) | copy-done | bytes 524312
  7.9 0.0 copy-start.6
  7.9 0.7 copy-done.6
  8.6 0.0 copy-start.7
  8.6 0.7 copy-done.7
  9.3 0.0 copy-start.8
  9.3 0.7 copy-done.8
  10.0 0.0 copy-start.9
  10.0 0.7 copy-done.9
  10.7 0.0 copy-start.10
  10.7 0.7 copy-done.10
  11.4 0.0 copy-start.11
  11.4 0.7 copy-done.11
  12.1 81.0 %window.1 = (bf16[16,32,512]{2,1,0:T(8,128)(2,1)S(1)}, f32[64,256]{1,0:T(8,128)S(1)}, f32[64,256]{1,0:T(8,128)S(1)}) custom-call(s32[1]{0:T(128)S(6)} %copy.21.shift_ref, bf16[16,32,512]{2,1,0:T(8,128)(2,1)S(1)} %copy-done.1, s32[16,32]{1,0:T(8,128)S(1)} %copy-done.7, f32[1,512]{1,0:T(1,128)S(1)} %bitcast.8, f32[1,512]{1,0:T(1,128)S(1)} %bitcast.9, ...), custom_call_target="tpu_custom_call" | custom-call | tf_op jit(solution)/shard_map/window/pallas_call | solution.py:612
  93.0 0.8 copy.22
  93.8 0.6 copy.23
  94.5 0.6 copy.24
Async XLA Ops:
  1.3 1.4 %copy-start = (bf16[512,1536]{1,0:T(8,128)(2,1)S(1)}, bf16[512,1536]{1,0:T(8,128)(2,1)}, u32[]{:S(2)}) copy-start(bf16[512,1536]{1,0:T(8,128)(2,1)} %qkv_hbm.1) | copy-start | bytes 4718596
  2.7 1.0 %copy-start.1 = (bf16[16,32,512]{2,1,0:T(8,128)(2,1)S(1)}, bf16[16,32,512]{2,1,0:T(8,128)(2,1)}, u32[]{:S(2)}) copy-start(bf16[16,32,512]{2,1,0:T(8,128)(2,1)} %features_ref.1) | copy-start | bytes 1572868
  3.7 1.0 %copy-start.2 = (bf16[16,32,512]{2,1,0:T(8,128)(2,1)S(1)}, bf16[16,32,512]{2,1,0:T(8,128)(2,1)}, u32[]{:S(2)}) copy-start(bf16[16,32,512]{2,1,0:T(8,128)(2,1)} %cotangent_ref.1) | copy-start | bytes 1572868
  4.8 1.0 %copy-start.3 = (bf16[512,512]{1,0:T(8,128)(2,1)S(1)}, bf16[512,512]{1,0:T(8,128)(2,1)}, u32[]{:S(2)}) copy-start(bf16[512,512]{1,0:T(8,128)(2,1)} %mix_hbm.1) | copy-start | bytes 1572868
  5.8 1.0 %copy-start.4 = (bf16[1024,256]{1,0:T(8,128)(2,1)S(1)}, bf16[1024,256]{1,0:T(8,128)(2,1)}, u32[]{:S(2)}) copy-start(bf16[1024,256]{1,0:T(8,128)(2,1)} %inner_hbm.1) | copy-start | bytes 1572868
  6.9 1.0 %copy-start.5 = (bf16[256,1024]{1,0:T(8,128)(2,1)S(1)}, bf16[256,1024]{1,0:T(8,128)(2,1)}, u32[]{:S(2)}) copy-start(bf16[256,1024]{1,0:T(8,128)(2,1)} %outer_hbm.1) | copy-start | bytes 1572868
  7.9 0.7 copy-start.6
  8.6 0.7 copy-start.7
  9.3 0.7 copy-start.8
  10.0 0.7 copy-start.9
  10.7 0.7 copy-start.10
  11.4 0.7 copy-start.11

commit v4 on v3

v4 whole, which is shorter than its diff:
```python
import jax
import jax.numpy as jnp
from jax import lax
from jax.experimental import pallas as pl
from jax.experimental.pallas import tpu as pltpu
from jax.sharding import PartitionSpec as P

HEADS1 = 8
WH = 8
WL = 16
D1 = 512
D2 = 1024
ROWS = 16
COLS = 32
CELLS = 128
HALF = 64
COPIES = 72
HIDDEN = 512

NORM_EPS = 1e-05
GELU_SCALE = 0.7978845608028654
MESH = pl.DeviceIdType.MESH
BF16 = jnp.bfloat16
F32 = jnp.float32
LAST = (((1,), (1,)), ((), ()))


def normalise(values):
    centre = jnp.mean(values, axis=-1, keepdims=True)
    centred = values - centre
    spread = jnp.mean(centred * centred, axis=-1, keepdims=True)
    return centred * lax.rsqrt(spread + NORM_EPS)


def gelu_pair(pre_act):
    square = pre_act * pre_act
    inner = GELU_SCALE * (pre_act + 0.044715 * square * pre_act)
    tangent = jnp.tanh(inner)
    half = 0.5 * (1.0 + tangent)
    value = pre_act * half
    slope = half + value * (1.0 - tangent) * (GELU_SCALE + (3.0 * 0.044715 * GELU_SCALE) * square)
    return (value, slope)


def matmul(a, b):
    return jnp.dot(a, b, preferred_element_type=F32)


def matmul_t(a, b):
    return lax.dot_general(a, b, LAST, preferred_element_type=F32)


class Copies:
    def __init__(self, send_sems, recv_sems):
        self.send_sems, self.recv_sems = send_sems, recv_sems
        self.places, self.started = {}, []

    def describe(self, name, src, dst, device):
        place = self.places.setdefault(name, len(self.places))
        return pltpu.make_async_remote_copy(
            src_ref=src,
            dst_ref=dst,
            send_sem=self.send_sems.at[place],
            recv_sem=self.recv_sems.at[place],
            device_id=device,
            device_id_type=MESH,
        )

    def start(self, name, src, dst, device):
        copy = self.describe(name, src, dst, device)
        copy.start()
        self.started.append(copy)

    def arrived(self, name, dst, device):
        self.describe(name, dst, dst, device).wait_recv()

    def finish(self):
        for copy in self.started:
            copy.wait_send()


def window_kernel(
    shift_ref, mask_ref, embed_ref, fine_gain_ref, table_ref, merge_gain_ref,
    coarse_gain_ref,
    features_hbm, cotangent_hbm, qkv_hbm, mix_hbm, merge_hbm, inner_hbm, outer_hbm, expand_hbm,
    prediction_ref, grad_inner_ref, grad_outer_ref,
    features_ref, cotangent_ref, qkv_ref, mix_ref, merge_ref, inner_ref, outer_ref, expand_ref,
    padded, table_rows, base, normed, halo, wide, bias, window, projected, attended, shifted, level, merged, coarse, back,
    lift, cots, part, core_in, x_in,
    hidden, slopes, hidden_t, cot_pre_t, sums, terms, y_in, ring_in, pair_in, side_out, side_in,
    load_sems, send_sems, recv_sems,
):
    lon, lat = lax.axis_index("lon"), lax.axis_index("lat")
    core, y_hi, x = lon % 2, (lon // 2) % 2, lon // 4
    z, y_lo = lat // 2, lat % 2
    east, west = {"lon": (lon + 1) % 16}, {"lon": (lon + 15) % 16}
    partner = {"lon": lon + 1 - 2 * core}
    across = {"lon": lon + 2 - 4 * y_hi}
    right, left = {"lon": (lon + 4) % 16}, {"lon": (lon + 12) % 16}
    opposite = {"lon": (lon + 8) % 16}
    up, down = {"lat": (lat + 2) % 16}, {"lat": (lat + 14) % 16}
    side = {"lat": lat + 1 - 2 * y_lo}

    loads, slots = {}, iter(range(12))

    def load(name, src, dst):
        loads[name] = pltpu.make_async_copy(src, dst, load_sems.at[next(slots)])
        loads[name].start()

    own = pl.ds(0, HIDDEN // 2)
    other = pl.ds(HIDDEN // 2, HIDDEN // 2)
    load("features", features_hbm, features_ref)
    load("cotangent", cotangent_hbm, cotangent_ref)
    for j in range(4):
        rows = pl.ds(j * 256, 256)
        load("expand%d" % j, expand_hbm.at[rows], expand_ref.at[rows])
    barrier = pltpu.get_barrier_semaphore()
    neighbours = (east, west, partner, across, right, left, opposite, up, down, side)
    for device in neighbours:
        pl.semaphore_signal(barrier, inc=1, device_id=device, device_id_type=MESH)

    loads["features"].wait()
    pl.semaphore_wait(barrier, len(neighbours))
    copies = Copies(send_sems, recv_sems)
    early, late = pl.ds(0, 256), pl.ds(256, D2 - 256)
    copies.start("inner0", inner_hbm.at[early], inner_ref.at[1, early], across)

    diagonal = lax.broadcasted_iota(jnp.int32, (COLS, COLS), 0) == lax.broadcasted_iota(
        jnp.int32, (COLS, COLS), 1
    )

    @pl.loop(0, ROWS, unroll=4)
    def _(r):
        land = mask_ref[pl.ds(r, 1), :].astype(F32)
        land = jnp.sum(jnp.where(diagonal, land, 0.0), axis=1, keepdims=True)
        cells = features_ref[r].astype(F32) + land * embed_ref[...]
        base[r] = cells
        rounded = (normalise(cells) * fine_gain_ref[...]).astype(BF16)
        normed[r] = rounded
        wide[r, WL : WL + COLS, :] = rounded.astype(F32)

    copies.start("halo e", normed.at[:, pl.ds(COLS - WL, WL), :], halo.at[0], east)
    copies.start("halo w", normed.at[:, pl.ds(0, WL), :], halo.at[1], west)

    padded[...] = jnp.zeros_like(padded)
    padded[:, 0 : table_ref.shape[1]] = table_ref[...]
    offsets = padded[...]
    top = offsets.astype(BF16)
    rest = offsets - top.astype(F32)
    middle = rest.astype(BF16)
    bottom = (rest - middle.astype(F32)).astype(BF16)
    turn = lax.broadcasted_iota(jnp.int32, (512, 640), 0) + lax.broadcasted_iota(
        jnp.int32, (512, 640), 1
    )
    turn = jnp.where(turn == table_ref.shape[1] - 1, 1.0, 0.0).astype(BF16)
    flipped = matmul(top, turn) + matmul(middle, turn) + matmul(bottom, turn)
    for i in range(2 * WH - 1):
        start = i * (2 * WL - 1)
        table_rows[i] = flipped[:, start : start + 128]
    lane = lax.broadcasted_iota(jnp.int32, (WL, 128), 1)

    @pl.loop(0, HEADS1)
    def _(h):
        halves = []
        for k in range(2):
            total = jnp.zeros((WL, 128), F32)
            for i in range(8 if k == 0 else 7):
                row = jnp.broadcast_to(table_rows[8 * k + i, pl.ds(h, 1), :], (WL, 128))
                turned = pltpu.roll(row, (128 - 15 + 16 * i) % 128, 1, stride=1, stride_axis=0)
                total = jnp.where(lane // 16 == i, turned, total)
            halves.append(total)
        both = jnp.concatenate(halves, axis=1)
        for i in range(WH):
            start = (WH - 1 - i) * WL
            bias[h, i * WL : (i + 1) * WL, :] = both[:, start : start + 128]

    def place(dx):
        return (0, 1, 3, 2)[dx % 4]

    def fold(store):
        @pl.loop(0, ROWS // 2, unroll=4)
        def _(r):
            store(
                r,
                [
                    jnp.concatenate(
                        [level[r, i, c, pl.ds(j, COLS // 2, stride=2), :] for c in range(4)], axis=1
                    )
                    for i in range(2)
                    for j in range(2)
                ],
            )

    loads["cotangent"].wait()

    @pl.loop(0, ROWS // 2)
    def _(r):
        for i in range(2):
            cells = cotangent_ref[2 * r + i].astype(F32)
            for c in range(4):
                level[r, i, c] = cells[:, c * 128 : (c + 1) * 128]

    def store_cot(r, quads):
        rows = pl.ds(pl.multiple_of(r * 16, 16), 16)
        for q in range(4):
            merged[rows, q * D1 : (q + 1) * D1] = quads[q].astype(BF16)

    fold(store_cot)
    for j in range(4):
        lanes = slice(j * 256, (j + 1) * 256)
        loads["expand%d" % j].wait()
        if j == 2:
            load("qkv", qkv_hbm, qkv_ref)
        cots[0, 0, :, lanes] = matmul_t(merged[...], expand_ref[lanes, :]).astype(BF16)

    load("mix", mix_hbm, mix_ref)
    load("merge", merge_hbm, merge_ref)
    load("inner", inner_hbm, inner_ref.at[0])
    load("outer", outer_hbm, outer_ref.at[own])

    front, rear = pl.ds(0, HALF), pl.ds(HALF, HALF)
    moves = {"r": (right, -1, 0), "l": (left, 1, 0), "o": (opposite, 2, 0), "p": (partner, 0, 1)}

    class Gather:
        def __init__(self, name, array):
            self.name, self.array = name, array

        def at(self, dx, rows=None, dk=0):
            block = self.array.at[place(dx), dk]
            return block if rows is None else block.at[rows]

        def send(self, name, dx, rows, way):
            device, mx, mk = moves[way]
            copies.start(self.name + name, self.at(dx, rows), self.at(dx + mx, rows, mk), device)

        def came(self, name, dx, rows, way):
            copies.arrived(self.name + name, self.at(dx, rows), moves[way][0])

        def share(self, dx):
            self.send("p%d" % dx, dx, None, "p")

        def shared(self, dx):
            copies.arrived(self.name + "p%d" % dx, self.at(dx, None, 1), partner)

    gather_cot, gather_lift = Gather("c", cots), Gather("l", lift)
    gather_cot.send("r", 0, None, "r")
    gather_cot.send("l", 0, None, "l")
    gather_cot.send("o", 0, None, "o")
    gather_cot.share(0)

    offset = shift_ref[0]
    first_head = lax.broadcasted_iota(jnp.int32, (CELLS, 128), 1) < 64
    ones = jnp.ones((CELLS, 128), BF16)

    def attend(w):
        @pl.loop(0, ROWS, unroll=4)
        def _(r):
            cells = wide[r, w * WL : (w + 2) * WL, :]
            window[r] = pltpu.roll(cells, 2 * WL - offset, 0)[:WL].astype(BF16)

        @pl.loop(0, 6, unroll=3)
        def _(j):
            lanes = pl.ds(pl.multiple_of(j * 256, 256), 256)
            rows = window[...].reshape(ROWS * WL, D1)
            projected[:, lanes] = matmul(rows, qkv_ref[:, lanes]).astype(BF16)

        @pl.loop(0, 8, unroll=8)
        def _(k):
            band, pair = k // 4, k % 4
            rows = pl.ds(pl.multiple_of(band * CELLS, CELLS), CELLS)

            def lanes(kind):
                return pl.ds(pl.multiple_of(kind * D1 + pair * 128, 128), 128)

            queries = projected[rows, lanes(0)] * 0.125
            zero = jnp.zeros_like(queries)
            queries = jnp.concatenate(
                [jnp.where(first_head, queries, zero), jnp.where(first_head, zero, queries)], axis=0
            )
            scores = matmul_t(queries, projected[rows, lanes(1)])
            scores = scores + bias[pl.ds(2 * pair, 2)].reshape(2 * CELLS, 128)
            expo = jnp.exp(scores - jnp.max(scores, axis=1, keepdims=True)).astype(BF16)
            values = jnp.concatenate([projected[rows, lanes(2)], ones], axis=1)
            sums = matmul(expo, values)
            heads = jnp.where(first_head, sums[:CELLS, :128], sums[CELLS:, :128]) / jnp.where(
                first_head, sums[:CELLS, 128:], sums[CELLS:, 128:]
            )
            attended[pl.ds(band * WH, WH), w * WL : (w + 1) * WL, lanes(0)] = heads.reshape(
                WH, WL, 128
            )

    loads["qkv"].wait()
    attend(1)
    copies.arrived("halo e", halo.at[0], east)
    copies.arrived("halo w", halo.at[1], west)

    @pl.loop(0, ROWS)
    def _(r):
        wide[r, 0:WL, :] = halo[0, r].astype(F32)
        wide[r, WL + COLS :, :] = halo[1, r].astype(F32)

    copies.start("inner1", inner_hbm.at[late], inner_ref.at[1, late], across)
    attend(0)
    attend(2)
    copies.start("outer", outer_hbm, outer_ref.at[other], across)

    loads["mix"].wait()

    @pl.loop(0, ROWS, unroll=4)
    def _(r):
        shifted[r] = pltpu.roll(attended[r], COLS + offset, 0)[:COLS].astype(BF16)

    @pl.loop(0, 2)
    def _(i):
        rows = pl.ds(i * 8, 8)
        mixed = matmul(shifted[rows].reshape(2 * CELLS, D1), mix_ref[...]).reshape(8, COLS, D1)
        mixed = (base[rows] + mixed).astype(BF16).astype(F32).reshape(4, 2, COLS, D1)
        for c in range(4):
            level[pl.ds(i * 4, 4), :, c] = mixed[..., c * 128 : (c + 1) * 128]

    def store_merged(r, quads):
        centre = sum(jnp.sum(quad, axis=1, keepdims=True) for quad in quads) / (4 * D1)
        quads = [quad - centre for quad in quads]
        spread = sum(jnp.sum(quad * quad, axis=1, keepdims=True) for quad in quads) / (4 * D1)
        scale = lax.rsqrt(spread + NORM_EPS)
        rows = pl.ds(pl.multiple_of(r * 16, 16), 16)
        for q in range(4):
            lanes = slice(q * D1, (q + 1) * D1)
            merged[rows, lanes] = (quads[q] * scale * merge_gain_ref[:, lanes]).astype(BF16)

    fold(store_merged)
    loads["merge"].wait()

    @pl.loop(0, 4)
    def _(j):
        lanes = pl.ds(pl.multiple_of(j * 256, 256), 256)
        coarse[:, lanes] = matmul(merged[...], merge_ref[:, lanes]).astype(BF16)

    @pl.loop(0, 4, unroll=4)
    def _(i):
        rows = pl.ds(pl.multiple_of(i * 32, 32), 32)
        lift[0, 0, rows, :] = (
            normalise(coarse[rows, :].astype(F32)) * coarse_gain_ref[...]
        ).astype(BF16)

    gather_lift.send("r0", 0, front, "r")
    gather_lift.send("l0", 0, rear, "l")
    gather_lift.send("r1", 0, rear, "r")
    gather_lift.send("l1", 0, front, "l")
    gather_lift.share(0)
    for way, dx in (("r", 3), ("l", 1), ("o", 2)):
        gather_cot.came(way, dx, None, way)
        gather_cot.share(dx)
    copies.arrived("inner0", inner_ref.at[1, early], across)
    copies.arrived("inner1", inner_ref.at[1, late], across)
    loads["inner"].wait()
    loads["outer"].wait()

    unit = lax.broadcasted_iota(jnp.int32, (256, 256), 0) == lax.broadcasted_iota(
        jnp.int32, (256, 256), 1
    )
    unit = jnp.where(unit, 1.0, 0.0).astype(BF16)

    def activate(dx):
        gather_lift.shared(dx)
        p = place(dx)
        columns = slice(p * 2 * CELLS, (p + 1) * 2 * CELLS)
        for half in range(2):
            rows = slice(half * 256, (half + 1) * 256)
            pre = matmul(lift[p].reshape(2 * CELLS, D2), inner_ref[half])
            value, slope = gelu_pair(pre)
            value = value.astype(BF16)
            hidden[p, :, rows] = value
            slopes[p, half] = slope
            hidden_t[rows, columns] = matmul_t(unit, value).astype(BF16)

    def project(dx):
        p = place(dx)
        part[p] = matmul(hidden[p], outer_ref[...]).astype(BF16).reshape(2, CELLS, D2)
        copies.start("s%d" % dx, part.at[p, 1], core_in.at[p], partner)

    def pull_back(dx):
        p = place(dx)
        columns = slice(p * 2 * CELLS, (p + 1) * 2 * CELLS)
        for half in range(2):
            rows = slice(half * 256, (half + 1) * 256)
            cot_hidden = matmul_t(cots[p].reshape(2 * CELLS, D2), outer_ref[rows, :])
            cot_pre = (cot_hidden * slopes[p, half]).astype(BF16)
            cot_pre_t[rows, columns] = matmul_t(unit, cot_pre).astype(BF16)

    def gradient(kind, begin, end):
        rows, array = ((cot_pre_t, lift), (hidden_t, cots))[kind]

        @pl.loop(0, 4)
        def _(j):
            lanes = pl.ds(pl.multiple_of(j * 256, 256), 256)
            cells = array[begin:end, :, :, lanes].reshape((end - begin) * 2 * CELLS, 256)
            term = matmul(rows[:, begin * 2 * CELLS : end * 2 * CELLS], cells)
            if begin > 0:
                term = term + sums[:, lanes]
            if end < 4:
                sums[:, lanes] = term
            else:
                for k in range(2):
                    half = term[:, k * 128 : (k + 1) * 128].astype(BF16)
                    terms[2 * j + k, kind] = half.reshape(2, 256, 128)

    def cores(dx):
        p = place(dx)
        copies.arrived("s%d" % dx, core_in.at[p], partner)
        part[p, 0] = (part[p, 0].astype(F32) + core_in[p].astype(F32)).astype(BF16)
        if dx > 0:
            device = {1: right, 3: left, 2: opposite}[dx]
            copies.start("t%d" % dx, part.at[p, 0], x_in.at[dx - 1], device)

    def zed(dz):
        return (z + dz) % 8

    ways = ((0, up, 1), (1, down, -1))
    thin = (pl.ds(0, 128), pl.ds(128, 128))

    def term_of(mine, chain):
        if chain < 2:
            return terms.at[mine, 1, chain]
        return terms.at[mine, 0, 0, thin[chain - 2]]

    def landing(step, way, chain):
        if chain < 2:
            return ring_in.at[step, way, 0, chain]
        return ring_in.at[step, way, 1, 0, thin[chain - 2]]

    def ring_send(step, way, chain):
        device, sign = ways[way][1:]
        mine = zed(sign * (4 - step) + 8)
        name = "z%d%d%d" % (step, way, chain)
        copies.start(name, term_of(mine, chain), landing(step, way, chain), device)

    def ring_begin(chain):
        ring_send(0, chain % 2, chain)

    def ring_other(chain):
        ring_send(1, 1 - chain % 2, chain)

    def ring_take(step, way, chain):
        here = landing(step, way, chain)
        copies.arrived("z%d%d%d" % (step, way, chain), here, ways[way][1])
        return here[...].astype(F32)

    def ring_step(step, chain):
        for way, device, sign in ways:
            if step == 1 and way != chain % 2:
                continue
            mine = term_of(zed(sign * (4 - step) + 8), chain)
            mine[...] = (mine[...].astype(F32) + ring_take(step - 1, way, chain)).astype(BF16)
            ring_send(step, way, chain)

    def ring_end(chain):
        total = term_of(z, chain)[...].astype(F32)
        return total + ring_take(3, 0, chain) + ring_take(3, 1, chain)

    order = (4, 3, 5, 2, 6, 1, 7, 0)

    def pair_begin():
        for d in order:
            copies.start("y%d" % d, terms.at[zed(d), 0, 1], y_in.at[d], across)

    def pair_add(d):
        copies.arrived("y%d" % d, y_in.at[d], across)
        mine = zed(d)
        terms[mine, 0, 0] = (terms[mine, 0, 0].astype(F32) + y_in[d].astype(F32)).astype(BF16)

    def side_begin(kind, total):
        side_out[kind] = total.T.reshape(2, HALF, 256)
        side_in[1, kind] = side_out[kind, 1 - y_lo].astype(BF16)
        copies.start("side%d" % kind, side_in.at[1, kind], side_in.at[0, kind], side)

    activate(0)
    for name, rows, dx, way in (("r0", front, 3, "r"), ("l0", rear, 1, "l")):
        gather_lift.came(name, dx, rows, way)
        gather_lift.send("f" + way, dx, rows, way)
    gather_lift.came("r1", 3, rear, "r")
    gather_lift.share(3)
    gather_lift.came("l1", 1, front, "l")
    gather_lift.share(1)
    activate(3)
    activate(1)
    for dx in (0, 3, 1, 2):
        gather_cot.shared(dx)
    gradient(1, 0, 3)
    gather_lift.came("fr", 2, front, "r")
    gather_lift.came("fl", 2, rear, "l")
    gather_lift.share(2)
    activate(2)
    gradient(1, 3, 4)
    ring_begin(0)
    ring_begin(1)
    ring_other(0)
    ring_other(1)
    copies.arrived("outer", outer_ref.at[other], across)
    project(2)
    project(3)
    project(1)
    project(0)
    cores(2)
    cores(3)
    cores(1)
    pull_back(0)
    pull_back(3)
    ring_step(1, 0)
    ring_step(1, 1)
    pull_back(1)
    pull_back(2)
    gradient(0, 0, 4)
    pair_begin()
    cores(0)
    ring_step(2, 0)
    ring_step(2, 1)
    pair_add(4)
    ring_begin(2)
    ring_begin(3)
    pair_add(3)
    pair_add(5)
    ring_other(2)
    ring_other(3)
    ring_step(3, 0)
    ring_step(3, 1)
    ring_step(1, 2)
    ring_step(1, 3)
    pair_add(2)
    pair_add(6)
    ring_step(2, 2)
    ring_step(2, 3)
    pair_in[1] = ring_end(1).astype(BF16)
    copies.start("pair", pair_in.at[1], pair_in.at[0], across)
    outer_total = ring_end(0)
    pair_add(1)
    pair_add(7)
    ring_step(3, 2)
    ring_step(3, 3)
    copies.arrived("pair", pair_in.at[0], across)
    side_begin(1, outer_total + pair_in[0].astype(F32))
    pair_add(0)

    update = part[0, 0].astype(F32)
    for dx, device in ((1, right), (3, left), (2, opposite)):
        copies.arrived("t%d" % dx, x_in.at[dx - 1], device)
        update = update + x_in[dx - 1].astype(F32)
    back[...] = (coarse[...].astype(F32) + update).astype(BF16)

    for q in range(4):
        raised = matmul(back[...], expand_ref[:, q * D1 : (q + 1) * D1])
        cells = pl.ds(q % 2, COLS // 2, stride=2)
        for c in range(4):
            block = raised[:, c * 128 : (c + 1) * 128].reshape(ROWS // 2, COLS // 2, 128)
            level[:, q // 2, c, cells, :] = level[:, q // 2, c, cells, :] + block

    @pl.loop(0, ROWS // 2)
    def _(r):
        for i in range(2):
            for c in range(4):
                prediction_ref[2 * r + i, :, c * 128 : (c + 1) * 128] = level[r, i, c].astype(BF16)

    side_begin(0, jnp.concatenate([ring_end(2), ring_end(3)], axis=0))
    for kind, out in ((1, grad_outer_ref), (0, grad_inner_ref)):
        copies.arrived("side%d" % kind, side_in.at[0, kind], side)
        out[...] = side_out[kind, y_lo] + side_in[0, kind].astype(F32)
    copies.finish()


def hand_over_kernel(*refs):
    for k in range(3):
        refs[3 + k][...] = refs[k][...]


def local(
    features, land_mask, land_embed, window_shift, fine_gain, qkv_weight, bias_table, mix_weight,
    merge_gain, merge_weight, coarse_gain, inner_weight, outer_weight, expand_weight, cotangent,
):
    vmem = pl.BlockSpec(memory_space=pltpu.VMEM)
    smem = pl.BlockSpec(memory_space=pltpu.SMEM)
    anywhere = pl.BlockSpec(memory_space=pl.ANY)
    wide_block = pltpu.VMEM((4, 2, CELLS, D2), BF16)
    outputs = pl.pallas_call(
        window_kernel,
        out_shape=(
            jax.ShapeDtypeStruct((ROWS, COLS, D1), BF16),
            jax.ShapeDtypeStruct((HALF, 256), F32),
            jax.ShapeDtypeStruct((HALF, 256), F32),
        ),
        in_specs=[smem] + [vmem] * 6 + [anywhere] * 8,
        out_specs=(vmem,) * 3,
        scratch_shapes=[
            pltpu.VMEM((ROWS, COLS, D1), BF16),
            pltpu.VMEM((ROWS, COLS, D1), BF16),
            pltpu.VMEM((D1, 3 * D1), BF16),
            pltpu.VMEM((D1, D1), BF16),
            pltpu.VMEM((4 * D1, D2), BF16),
            pltpu.VMEM((2, D2, HIDDEN // 2), BF16),
            pltpu.VMEM((HIDDEN, D2), BF16),
            pltpu.VMEM((D2, 4 * D1), BF16),
            pltpu.VMEM((HEADS1, 512), F32),
            pltpu.VMEM((2 * WH - 1, HEADS1, 128), F32),
            pltpu.VMEM((ROWS, COLS, D1), F32),
            pltpu.VMEM((ROWS, COLS, D1), BF16),
            pltpu.VMEM((2, ROWS, WL, D1), BF16),
            pltpu.VMEM((ROWS, COLS + 2 * WL, D1), F32),
            pltpu.VMEM((HEADS1, CELLS, CELLS), F32),
            pltpu.VMEM((ROWS, WL, D1), BF16),
            pltpu.VMEM((ROWS * WL, 3 * D1), BF16),
            pltpu.VMEM((ROWS, COLS + WL, D1), F32),
            pltpu.VMEM((ROWS, COLS, D1), BF16),
            pltpu.VMEM((ROWS // 2, 2, 4, COLS, 128), F32),
            pltpu.VMEM((CELLS, 4 * D1), BF16),
            pltpu.VMEM((CELLS, D2), BF16),
            pltpu.VMEM((CELLS, D2), BF16),
            wide_block,
            wide_block,
            wide_block,
            pltpu.VMEM((4, CELLS, D2), BF16),
            pltpu.VMEM((3, CELLS, D2), BF16),
            pltpu.VMEM((4, 2 * CELLS, HIDDEN), BF16),
            pltpu.VMEM((4, 2, 2 * CELLS, 256), F32),
            pltpu.VMEM((HIDDEN, 8 * CELLS), BF16),
            pltpu.VMEM((HIDDEN, 8 * CELLS), BF16),
            pltpu.VMEM((HIDDEN, D2), F32),
            pltpu.VMEM((8, 2, 2, 256, 128), BF16),
            pltpu.VMEM((8, 256, 128), BF16),
            pltpu.VMEM((4, 2, 2, 2, 256, 128), BF16),
            pltpu.VMEM((2, 256, 128), BF16),
            pltpu.VMEM((2, 2, HALF, 256), F32),
            pltpu.VMEM((2, 2, HALF, 256), BF16),
            pltpu.SemaphoreType.DMA((12,)),
            pltpu.SemaphoreType.DMA((COPIES,)),
            pltpu.SemaphoreType.DMA((COPIES,)),
        ],
        compiler_params=pltpu.CompilerParams(
            collective_id=0, has_side_effects=True, vmem_limit_bytes=56 * 1024 * 1024
        ),
        name="window",
    )(
        window_shift, land_mask, land_embed[None], fine_gain[None], bias_table,
        merge_gain[None], coarse_gain[None], features, cotangent,
        qkv_weight, mix_weight, merge_weight, inner_weight, outer_weight, expand_weight,
    )
    prediction, grad_inner, grad_outer = pl.pallas_call(
        hand_over_kernel,
        out_shape=tuple(jax.ShapeDtypeStruct(x.shape, x.dtype) for x in outputs),
        in_specs=[vmem] * 3,
        out_specs=(vmem,) * 3,
        name="hand_over",
    )(*outputs)
    return prediction, grad_inner, grad_outer.T


def solution(mesh):
    return jax.shard_map(
        local,
        mesh=mesh,
        in_specs=(
            P("lat", "lon", None),
            P("lat", "lon"),
            P(),
            P(),
            P(),
            P(),
            P(),
            P(),
            P(),
            P(),
            P(),
            P(None, "lon"),
            P("lon", None),
            P(),
            P("lat", "lon", None),
        ),
        out_specs=(P("lat", "lon", None), P("lat", "lon"), P("lon", "lat")),
        check_vma=False,
    )
```

time: 95.7 us -> 81.5 us (0.85)
  local copies, waits for them, and re-layouts: 12.8 us -> 0 us
  Pallas kernels: 81 us -> 80 us
    unnamed x27 -> x0, local copies, waits for them, and re-layouts: 12.8 us -> none
    pallas_call x1, Pallas kernels: 81 us -> 78.1 us  [local(): pl.pallas_call(window_kernel, out_shape=(jax.ShapeDtypeStruct((ROWS, COLS...]
    pallas_call x0 -> x1, Pallas kernels: none -> 1.93 us  [local(): pl.pallas_call(hand_over_kernel, out_shape=tuple((jax.ShapeDtypeStruct(x....]
where the time goes in v4:
time: 81.5 us; the launch traced here: 81.3 us
  Pallas kernels  80 us (98%)
  between operations  1.29 us (2%)
    pallas_call x1, Pallas kernels, local(): pl.pallas_call(window_kernel, out_shape=(jax.ShapeDtypeStruct((ROWS, COLS...  78.1 us
    pallas_call x1, Pallas kernels, local(): pl.pallas_call(hand_over_kernel, out_shape=tuple((jax.ShapeDtypeStruct(x....  1.93 us

profile of v4, /device:TPU:8, one launch (start us, length us, event | category | flops | bytes accessed | tf_op | source)
XLA Modules:
  0.0 81.3 jit_solution(12879122119883423203)
XLA Ops:
  1.3 78.1 %window.1 = (bf16[16,32,512]{2,1,0:T(8,128)(2,1)}, f32[64,256]{1,0:T(8,128)}, f32[64,256]{1,0:T(8,128)}) custom-call(s32[1]{0:T(128)S(6)} %copy.18.shift_ref, s32[16,32]{1,0:T(8,128)} %mask_ref.1, f32[1,512]{1,0:T(1,128)} %bitcast.7, f32[1,512]{1,0:T(1,128)} %bitcast.8, f32[8,465]{1,0:T(8,128)} %table_ref.1, f32[1,2048]{1,0:T(1,128)} %bitcast.5, ...), custom_call_target="tpu_custom_call" | custom-call | tf_op jit(solution)/shard_map/window/pallas_call | solution.py:583
  79.4 1.9 %hand_over.1 = (bf16[16,32,512]{2,1,0:T(8,128)(2,1)}, f32[64,256]{1,0:T(8,128)}, f32[64,256]{1,0:T(8,128)}) custom-call(bf16[16,32,512]{2,1,0:T(8,128)(2,1)} %get-tuple-element.9.refs_0_, f32[64,256]{1,0:T(8,128)} %get-tuple-element.10.refs_1_, f32[64,256]{1,0:T(8,128)} %get-tuple-element.11.refs_2_), custom_call_target="tpu_custom_call" | custom-call | tf_op jit(solution)/shard_map/hand_over/pallas_call | solution.py:645

commit v5 on v4

--- a/solution.py
+++ b/solution.py
@@ -87,7 +87,7 @@
     features_ref, cotangent_ref, qkv_ref, mix_ref, merge_ref, inner_ref, outer_ref, expand_ref,
     padded, table_rows, base, normed, halo, wide, bias, window, projected, attended, shifted, level, merged, coarse, back,
     lift, cots, part, core_in, x_in,
-    hidden, slopes, hidden_t, cot_pre_t, sums, terms, y_in, ring_in, pair_in, side_out, side_in,
+    hidden, slopes, hidden_t, cot_pre_t, sums, terms, y_in, ring_in, side_out, side_in, corner_out, corner_in,
     load_sems, send_sems, recv_sems,
 ):
     lon, lat = lax.axis_index("lon"), lax.axis_index("lat")
@@ -100,6 +100,7 @@
     opposite = {"lon": (lon + 8) % 16}
     up, down = {"lat": (lat + 2) % 16}, {"lat": (lat + 14) % 16}
     side = {"lat": lat + 1 - 2 * y_lo}
+    corner = {"lat": lat + 1 - 2 * y_lo, "lon": lon + 2 - 4 * y_hi}
 
     loads, slots = {}, iter(range(12))
 
@@ -115,7 +116,7 @@
         rows = pl.ds(j * 256, 256)
         load("expand%d" % j, expand_hbm.at[rows], expand_ref.at[rows])
     barrier = pltpu.get_barrier_semaphore()
-    neighbours = (east, west, partner, across, right, left, opposite, up, down, side)
+    neighbours = (east, west, partner, across, right, left, opposite, up, down, side, corner)
     for device in neighbours:
         pl.semaphore_signal(barrier, inc=1, device_id=device, device_id_type=MESH)
 
@@ -379,31 +380,30 @@
         part[p] = matmul(hidden[p], outer_ref[...]).astype(BF16).reshape(2, CELLS, D2)
         copies.start("s%d" % dx, part.at[p, 1], core_in.at[p], partner)
 
-    def pull_back(dx):
-        p = place(dx)
-        columns = slice(p * 2 * CELLS, (p + 1) * 2 * CELLS)
-        for half in range(2):
-            rows = slice(half * 256, (half + 1) * 256)
+    def pull_back(half):
+        rows = slice(half * 256, (half + 1) * 256)
+        for p in range(4):
+            columns = slice(p * 2 * CELLS, (p + 1) * 2 * CELLS)
             cot_hidden = matmul_t(cots[p].reshape(2 * CELLS, D2), outer_ref[rows, :])
             cot_pre = (cot_hidden * slopes[p, half]).astype(BF16)
             cot_pre_t[rows, columns] = matmul_t(unit, cot_pre).astype(BF16)
 
-    def gradient(kind, begin, end):
-        rows, array = ((cot_pre_t, lift), (hidden_t, cots))[kind]
+    def gradient(kind, half, begin, end):
+        left_ref, array = ((cot_pre_t, lift), (hidden_t, cots))[kind]
+        rows = slice(half * 256, (half + 1) * 256)
 
         @pl.loop(0, 4)
         def _(j):
             lanes = pl.ds(pl.multiple_of(j * 256, 256), 256)
             cells = array[begin:end, :, :, lanes].reshape((end - begin) * 2 * CELLS, 256)
-            term = matmul(rows[:, begin * 2 * CELLS : end * 2 * CELLS], cells)
+            term = matmul(left_ref[rows, begin * 2 * CELLS : end * 2 * CELLS], cells)
             if begin > 0:
-                term = term + sums[:, lanes]
+                term = term + sums[rows, lanes]
             if end < 4:
-                sums[:, lanes] = term
+                sums[rows, lanes] = term
             else:
                 for k in range(2):
-                    half = term[:, k * 128 : (k + 1) * 128].astype(BF16)
-                    terms[2 * j + k, kind] = half.reshape(2, 256, 128)
+                    terms[2 * j + k, kind, half] = term[:, k * 128 : (k + 1) * 128].astype(BF16)
 
     def cores(dx):
         p = place(dx)
@@ -460,19 +460,32 @@
 
     order = (4, 3, 5, 2, 6, 1, 7, 0)
 
-    def pair_begin():
-        for d in order:
-            copies.start("y%d" % d, terms.at[zed(d), 0, 1], y_in.at[d], across)
+    def pair_send(d):
+        copies.start("y%d" % d, terms.at[zed(d), 0, 1], y_in.at[d], across)
 
     def pair_add(d):
         copies.arrived("y%d" % d, y_in.at[d], across)
+        later = order.index(d) + 4
+        if later < 8:
+            pair_send(order[later])
         mine = zed(d)
         terms[mine, 0, 0] = (terms[mine, 0, 0].astype(F32) + y_in[d].astype(F32)).astype(BF16)
 
-    def side_begin(kind, total):
-        side_out[kind] = total.T.reshape(2, HALF, 256)
-        side_in[1, kind] = side_out[kind, 1 - y_lo].astype(BF16)
-        copies.start("side%d" % kind, side_in.at[1, kind], side_in.at[0, kind], side)
+    def side_begin(total):
+        side_out[0] = total.T.reshape(2, HALF, 256)
+        side_in[1] = side_out[0, 1 - y_lo].astype(BF16)
+        copies.start("side", side_in.at[1], side_in.at[0], side)
+
+    corners = ((0, 1, side), (1, 0, across), (1, 1, corner))
+
+    def corners_begin():
+        totals = [ring_end(0), ring_end(1)]
+        for half in range(2):
+            side_out[1 + half] = totals[half].T.reshape(2, HALF, 256)
+        for k, (half, turn, device) in enumerate(corners):
+            row = 1 - y_lo if turn else y_lo
+            corner_out[k] = side_out[1 + half, row].astype(BF16)
+            copies.start("corner%d" % k, corner_out.at[k], corner_in.at[k], device)
 
     activate(0)
     for name, rows, dx, way in (("r0", front, 3, "r"), ("l0", rear, 1, "l")):
@@ -486,17 +499,25 @@
     activate(1)
     for dx in (0, 3, 1, 2):
         gather_cot.shared(dx)
-    gradient(1, 0, 3)
+    gradient(1, 0, 0, 3)
+    gradient(1, 1, 0, 3)
     gather_lift.came("fr", 2, front, "r")
     gather_lift.came("fl", 2, rear, "l")
     gather_lift.share(2)
     activate(2)
-    gradient(1, 3, 4)
+    gradient(1, 0, 3, 4)
     ring_begin(0)
+    ring_other(0)
+    gradient(1, 1, 3, 4)
     ring_begin(1)
-    ring_other(0)
     ring_other(1)
     copies.arrived("outer", outer_ref.at[other], across)
+    pull_back(1)
+    gradient(0, 1, 0, 4)
+    for d in order[:4]:
+        pair_send(d)
+    ring_step(1, 0)
+    ring_step(1, 1)
     project(2)
     project(3)
     project(1)
@@ -504,17 +525,11 @@
     cores(2)
     cores(3)
     cores(1)
-    pull_back(0)
-    pull_back(3)
-    ring_step(1, 0)
-    ring_step(1, 1)
-    pull_back(1)
-    pull_back(2)
-    gradient(0, 0, 4)
-    pair_begin()
-    cores(0)
     ring_step(2, 0)
     ring_step(2, 1)
+    pull_back(0)
+    gradient(0, 0, 0, 4)
+    cores(0)
     pair_add(4)
     ring_begin(2)
     ring_begin(3)
@@ -530,15 +545,11 @@
     pair_add(6)
     ring_step(2, 2)
     ring_step(2, 3)
-    pair_in[1] = ring_end(1).astype(BF16)
-    copies.start("pair", pair_in.at[1], pair_in.at[0], across)
-    outer_total = ring_end(0)
+    corners_begin()
     pair_add(1)
     pair_add(7)
     ring_step(3, 2)
     ring_step(3, 3)
-    copies.arrived("pair", pair_in.at[0], across)
-    side_begin(1, outer_total + pair_in[0].astype(F32))
     pair_add(0)
 
     update = part[0, 0].astype(F32)
@@ -560,10 +571,14 @@
             for c in range(4):
                 prediction_ref[2 * r + i, :, c * 128 : (c + 1) * 128] = level[r, i, c].astype(BF16)
 
-    side_begin(0, jnp.concatenate([ring_end(2), ring_end(3)], axis=0))
-    for kind, out in ((1, grad_outer_ref), (0, grad_inner_ref)):
-        copies.arrived("side%d" % kind, side_in.at[0, kind], side)
-        out[...] = side_out[kind, y_lo] + side_in[0, kind].astype(F32)
+    side_begin(jnp.concatenate([ring_end(2), ring_end(3)], axis=0))
+    total = side_out[1, y_lo]
+    for k, (half, turn, device) in enumerate(corners):
+        copies.arrived("corner%d" % k, corner_in.at[k], device)
+        total = total + corner_in[k].astype(F32)
+    grad_outer_ref[...] = total
+    copies.arrived("side", side_in.at[0], side)
+    grad_inner_ref[...] = side_out[0, y_lo] + side_in[0].astype(F32)
     copies.finish()
 
 
@@ -626,9 +641,10 @@
             pltpu.VMEM((8, 2, 2, 256, 128), BF16),
             pltpu.VMEM((8, 256, 128), BF16),
             pltpu.VMEM((4, 2, 2, 2, 256, 128), BF16),
-            pltpu.VMEM((2, 256, 128), BF16),
-            pltpu.VMEM((2, 2, HALF, 256), F32),
-            pltpu.VMEM((2, 2, HALF, 256), BF16),
+            pltpu.VMEM((3, 2, HALF, 256), F32),
+            pltpu.VMEM((2, HALF, 256), BF16),
+            pltpu.VMEM((3, HALF, 256), BF16),
+            pltpu.VMEM((3, HALF, 256), BF16),
             pltpu.SemaphoreType.DMA((12,)),
             pltpu.SemaphoreType.DMA((COPIES,)),
             pltpu.SemaphoreType.DMA((COPIES,)),

time: 81.5 us -> 78.1 us (0.958)
  Pallas kernels: 80 us -> 76.6 us
    pallas_call x1, Pallas kernels: 78.1 us -> 74.7 us  [local(): pl.pallas_call(window_kernel, out_shape=(jax.ShapeDtypeStruct((ROWS, COLS...]
where the time goes in v5:
time: 78.1 us; the launch traced here: 77.9 us
  Pallas kernels  76.6 us (98%)
  between operations  1.29 us (2%)
    pallas_call x1, Pallas kernels, local(): pl.pallas_call(window_kernel, out_shape=(jax.ShapeDtypeStruct((ROWS, COLS...  74.7 us
    pallas_call x1, Pallas kernels, local(): pl.pallas_call(hand_over_kernel, out_shape=tuple((jax.ShapeDtypeStruct(x....  1.93 us

profile of v5, /device:TPU:8, one launch (start us, length us, event | category | flops | bytes accessed | tf_op | source)
XLA Modules:
  0.0 77.9 jit_solution(16188114381702871653)
XLA Ops:
  1.3 74.7 %window.1 = (bf16[16,32,512]{2,1,0:T(8,128)(2,1)}, f32[64,256]{1,0:T(8,128)}, f32[64,256]{1,0:T(8,128)}) custom-call(s32[1]{0:T(128)S(6)} %copy.18.shift_ref, s32[16,32]{1,0:T(8,128)} %mask_ref.1, f32[1,512]{1,0:T(1,128)} %bitcast.7, f32[1,512]{1,0:T(1,128)} %bitcast.8, f32[8,465]{1,0:T(8,128)} %table_ref.1, f32[1,2048]{1,0:T(1,128)} %bitcast.5, ...), custom_call_target="tpu_custom_call" | custom-call | tf_op jit(solution)/shard_map/window/pallas_call | solution.py:598
  76.0 1.9 %hand_over.1 = (bf16[16,32,512]{2,1,0:T(8,128)(2,1)}, f32[64,256]{1,0:T(8,128)}, f32[64,256]{1,0:T(8,128)}) custom-call(bf16[16,32,512]{2,1,0:T(8,128)(2,1)} %get-tuple-element.9.refs_0_, f32[64,256]{1,0:T(8,128)} %get-tuple-element.10.refs_1_, f32[64,256]{1,0:T(8,128)} %get-tuple-element.11.refs_2_), custom_call_target="tpu_custom_call" | custom-call | tf_op jit(solution)/shard_map/hand_over/pallas_call | solution.py:661

commit v6 on v5

--- a/solution.py
+++ b/solution.py
@@ -160,7 +160,7 @@
         table_rows[i] = flipped[:, start : start + 128]
     lane = lax.broadcasted_iota(jnp.int32, (WL, 128), 1)
 
-    @pl.loop(0, HEADS1)
+    @pl.loop(0, HEADS1, unroll=4)
     def _(h):
         halves = []
         for k in range(2):
@@ -295,7 +295,7 @@
     copies.arrived("halo e", halo.at[0], east)
     copies.arrived("halo w", halo.at[1], west)
 
-    @pl.loop(0, ROWS)
+    @pl.loop(0, ROWS, unroll=4)
     def _(r):
         wide[r, 0:WL, :] = halo[0, r].astype(F32)
         wide[r, WL + COLS :, :] = halo[1, r].astype(F32)
@@ -311,7 +311,7 @@
     def _(r):
         shifted[r] = pltpu.roll(attended[r], COLS + offset, 0)[:COLS].astype(BF16)
 
-    @pl.loop(0, 2)
+    @pl.loop(0, 2, unroll=2)
     def _(i):
         rows = pl.ds(i * 8, 8)
         mixed = matmul(shifted[rows].reshape(2 * CELLS, D1), mix_ref[...]).reshape(8, COLS, D1)
@@ -332,7 +332,7 @@
     fold(store_merged)
     loads["merge"].wait()
 
-    @pl.loop(0, 4)
+    @pl.loop(0, 4, unroll=4)
     def _(j):
         lanes = pl.ds(pl.multiple_of(j * 256, 256), 256)
         coarse[:, lanes] = matmul(merged[...], merge_ref[:, lanes]).astype(BF16)
@@ -392,7 +392,7 @@
         left_ref, array = ((cot_pre_t, lift), (hidden_t, cots))[kind]
         rows = slice(half * 256, (half + 1) * 256)
 
-        @pl.loop(0, 4)
+        @pl.loop(0, 4, unroll=4)
         def _(j):
             lanes = pl.ds(pl.multiple_of(j * 256, 256), 256)
             cells = array[begin:end, :, :, lanes].reshape((end - begin) * 2 * CELLS, 256)
@@ -565,7 +565,7 @@
             block = raised[:, c * 128 : (c + 1) * 128].reshape(ROWS // 2, COLS // 2, 128)
             level[:, q // 2, c, cells, :] = level[:, q // 2, c, cells, :] + block
 
-    @pl.loop(0, ROWS // 2)
+    @pl.loop(0, ROWS // 2, unroll=4)
     def _(r):
         for i in range(2):
             for c in range(4):

time: 78.1 us -> 75.2 us (0.963)
  Pallas kernels: 76.6 us -> 73.7 us
    pallas_call x1, Pallas kernels: 74.7 us -> 71.8 us  [local(): pl.pallas_call(window_kernel, out_shape=(jax.ShapeDtypeStruct((ROWS, COLS...]
where the time goes in v6:
time: 75.2 us; the launch traced here: 75 us
  Pallas kernels  73.7 us (98%)
  between operations  1.29 us (2%)
    pallas_call x1, Pallas kernels, local(): pl.pallas_call(window_kernel, out_shape=(jax.ShapeDtypeStruct((ROWS, COLS...  71.8 us
    pallas_call x1, Pallas kernels, local(): pl.pallas_call(hand_over_kernel, out_shape=tuple((jax.ShapeDtypeStruct(x....  1.93 us

profile of v6, /device:TPU:8, one launch (start us, length us, event | category | flops | bytes accessed | tf_op | source)
XLA Modules:
  0.0 75.0 jit_solution(1469777800423298564)
XLA Ops:
  1.3 71.8 %window.1 = (bf16[16,32,512]{2,1,0:T(8,128)(2,1)}, f32[64,256]{1,0:T(8,128)}, f32[64,256]{1,0:T(8,128)}) custom-call(s32[1]{0:T(128)S(6)} %copy.18.shift_ref, s32[16,32]{1,0:T(8,128)} %mask_ref.1, f32[1,512]{1,0:T(1,128)} %bitcast.7, f32[1,512]{1,0:T(1,128)} %bitcast.8, f32[8,465]{1,0:T(8,128)} %table_ref.1, f32[1,2048]{1,0:T(1,128)} %bitcast.5, ...), custom_call_target="tpu_custom_call" | custom-call | tf_op jit(solution)/shard_map/window/pallas_call | solution.py:598
  73.1 1.9 %hand_over.1 = (bf16[16,32,512]{2,1,0:T(8,128)(2,1)}, f32[64,256]{1,0:T(8,128)}, f32[64,256]{1,0:T(8,128)}) custom-call(bf16[16,32,512]{2,1,0:T(8,128)(2,1)} %get-tuple-element.9.refs_0_, f32[64,256]{1,0:T(8,128)} %get-tuple-element.10.refs_1_, f32[64,256]{1,0:T(8,128)} %get-tuple-element.11.refs_2_), custom_call_target="tpu_custom_call" | custom-call | tf_op jit(solution)/shard_map/hand_over/pallas_call | solution.py:661
